TPU v7x, 128 devices: a whole 4x4x4 slice. The times are simulated.
128 devices in a mesh: dp: 4 (over z), expert: 32 (over y, x, core).
Axes of the slice: x: 4, y: 4, z: 4, core: 2. Of those that a mesh axis runs over, the one named last changes fastest.
Arguments:
- tokens: bfloat16 [32768, 4096], P(('dp', 'expert')), may hold values from -6 to 6
- grad_out: bfloat16 [32768, 4096], P(('dp', 'expert')), may hold values from -6 to 6
- expert_ids: int32 [32768, 2], P(('dp', 'expert')), may hold values from 0 to 31, all different within a row; in each aligned block of 256 rows (0 to 255, 256 to 511, ...) at most 24 rows name the same one
- combine: bfloat16 [32768, 2], P(('dp', 'expert')), may hold values from 0.099609375 to 1
- w_gate: bfloat16 [32, 4096, 512], P('expert'), may hold values from -0.09375 to 0.09375
- w_up: bfloat16 [32, 4096, 512], P('expert'), may hold values from -0.09375 to 0.09375
- w_down: bfloat16 [32, 512, 4096], P('expert'), may hold values from -0.25 to 0.25
Outputs:
- grad_tokens: bfloat16 [32768, 4096], P(('dp', 'expert'))
- grad_combine: bfloat16 [32768, 2], P(('dp', 'expert'))
- grad_gate: bfloat16 [32, 4096, 512], P('expert', 'dp')
- grad_up: bfloat16 [32, 4096, 512], P('expert', 'dp')
- grad_down: bfloat16 [32, 512, 4096], P('expert', None, 'dp')
Inputs may be any that keep to these rules, and one draw needn't show every extreme that they name: `expert_ids`: the two experts of a token differ. In each aligned block of 256 rows (the rows of one device) no expert is named more than 24 times, a bound that some block reaches.
All inputs are finite; a program needn't handle non-finite values.
Results may differ from a plain program's by a relative error of at most 0.011.
Values may be sent and summed in bfloat16 or wider, within the bound.
A program may use at most 192 MiB of HBM per device.

v0:
```python
import jax
import jax.numpy as jnp
from jax import lax
from jax.sharding import PartitionSpec as P


def contract(left, right, left_dim, right_dim):
    return lax.dot_general(
        left, right, (((left_dim,), (right_dim,)), ((), ())), preferred_element_type=jnp.float32
    )


def local_places(expert_ids, capacity, experts):
    flat_ids = expert_ids.reshape(-1)
    labels = jnp.arange(experts, dtype=jnp.int32)
    hits = (flat_ids[:, None] == labels[None, :]).astype(jnp.int32)
    earlier = jnp.cumsum(hits, axis=0) - hits
    slot = jnp.sum(earlier * hits, axis=1)
    return flat_ids * capacity + slot


def expert_backward(rows_x, rows_dy, rows_p, gate_w, up_w, down_w):
    gate = jnp.dot(rows_x, gate_w, preferred_element_type=jnp.float32)
    upper = jnp.dot(rows_x, up_w, preferred_element_type=jnp.float32)
    sigma = jax.nn.sigmoid(gate)
    swish = gate * sigma
    hidden = (swish * upper).astype(jnp.bfloat16)
    hidden_grad = contract(rows_dy, down_w, 1, 1)
    combine_grad = jnp.sum(hidden.astype(jnp.float32) * hidden_grad, axis=1).astype(jnp.bfloat16)
    weight = rows_p.astype(jnp.float32)[:, None]
    scaled_grad = weight * hidden_grad
    gate_grad = (scaled_grad * upper * sigma * (1.0 + gate * (1.0 - sigma))).astype(jnp.bfloat16)
    up_grad = (scaled_grad * swish).astype(jnp.bfloat16)
    scaled_hidden = (weight * hidden.astype(jnp.float32)).astype(jnp.bfloat16)
    pick_grad = (contract(gate_grad, gate_w, 1, 1) + contract(up_grad, up_w, 1, 1)).astype(
        jnp.bfloat16
    )
    return (pick_grad, combine_grad, gate_grad, up_grad, scaled_hidden)


def on_device(tokens, grad_out, expert_ids, combine, w_gate, w_up, w_down):
    tok_rows = tokens.shape[0]
    width = tokens.shape[1]
    experts = lax.axis_size("expert")
    capacity = 3 * tok_rows // experts
    picks = 2 * tok_rows
    places = local_places(expert_ids, capacity, experts)
    filler = (
        jnp.full((experts * capacity,), picks, jnp.int32)
        .at[places]
        .set(jnp.arange(picks, dtype=jnp.int32))
    )
    owner = filler // 2
    zero_row = jnp.zeros((1, width), jnp.bfloat16)
    send_x = jnp.concatenate([tokens, zero_row], axis=0)[owner].reshape(experts, capacity, width)
    send_dy = jnp.concatenate([grad_out, zero_row], axis=0)[owner].reshape(experts, capacity, width)
    weights_ext = jnp.concatenate([combine.reshape(-1), jnp.zeros((1,), jnp.bfloat16)], axis=0)
    send_p = weights_ext[filler].reshape(experts, capacity)
    recv_x, recv_dy, recv_p = (
        lax.all_to_all(send_x, "expert", split_axis=0, concat_axis=0, tiled=True),
        lax.all_to_all(send_dy, "expert", split_axis=0, concat_axis=0, tiled=True),
        lax.all_to_all(send_p, "expert", split_axis=0, concat_axis=0, tiled=True),
    )
    rows_x = recv_x.reshape(-1, width)
    rows_dy = recv_dy.reshape(-1, width)
    outs = expert_backward(rows_x, rows_dy, recv_p.reshape(-1), w_gate[0], w_up[0], w_down[0])
    pick_grad, combine_grad, gate_grad, up_grad, scaled_hidden = outs
    back_rows, back_weights = (
        lax.all_to_all(
            pick_grad.reshape(experts, capacity, width),
            "expert",
            split_axis=0,
            concat_axis=0,
            tiled=True,
        ),
        lax.all_to_all(
            combine_grad.reshape(experts, capacity),
            "expert",
            split_axis=0,
            concat_axis=0,
            tiled=True,
        ),
    )
    pairs = back_rows.reshape(-1, width)[places].astype(jnp.float32).reshape(tok_rows, 2, width)
    grad_tokens = jnp.sum(pairs, axis=1).astype(jnp.bfloat16)
    grad_combine = back_weights.reshape(-1)[places].reshape(tok_rows, 2)
    gate_part = contract(rows_x, gate_grad, 0, 0)[None]
    up_part = contract(rows_x, up_grad, 0, 0)[None]
    down_part = contract(scaled_hidden, rows_dy, 0, 0)[None]
    gate_sum, up_sum, down_sum = (
        lax.psum_scatter(gate_part, "dp", scatter_dimension=1, tiled=True),
        lax.psum_scatter(up_part, "dp", scatter_dimension=1, tiled=True),
        lax.psum_scatter(down_part, "dp", scatter_dimension=2, tiled=True),
    )
    return (
        grad_tokens,
        grad_combine,
        gate_sum.astype(jnp.bfloat16),
        up_sum.astype(jnp.bfloat16),
        down_sum.astype(jnp.bfloat16),
    )


def solution(mesh):
    return jax.shard_map(
        on_device,
        mesh=mesh,
        in_specs=(
            P(("dp", "expert"), None),
            P(("dp", "expert"), None),
            P(("dp", "expert"), None),
            P(("dp", "expert"), None),
            P("expert", None, None),
            P("expert", None, None),
            P("expert", None, None),
        ),
        out_specs=(
            P(("dp", "expert"), None),
            P(("dp", "expert"), None),
            P("expert", "dp", None),
            P("expert", "dp", None),
            P("expert", None, "dp"),
        ),
        check_vma=False,
    )
```

profile of v0, /device:TPU:67, one launch (start us, length us, event | category | flops | bytes accessed | tf_op | source)
XLA Modules:
  0.0 471.5 jit_solution(8375075823274728081)
XLA Ops:
  7.2 0.7 broadcast_multiply_fusion
  7.9 0.8 copy.20
  8.7 0.1 eq.29
  8.8 0.1 eq.25
  9.0 0.8 copy.18
  9.8 0.1 reshape.114
  9.9 0.1 copy.19
  10.1 0.1 mul.59
  10.2 1.2 reduce-window.6
  11.4 0.2 slice_reduce_fusion
  11.7 0.1 fusion.16
  11.8 2.4 scatter_custom_fusion
  14.3 5.0 %gather_fusion = bf16[768]{0:T(1024)(128)(2,1)S(1)} fusion(bf16[513]{0:T(1024)(128)(2,1)S(1)} %pad_maximum_fusion, s32[1024]{0:T(1024)S(1)} %get-tuple-element.22), kind=kCustom, calls=%fused_computation | custom fusion | bytes 6144 | tf_op jit(solution)/shard_map/gather | solution.py:58
  19.3 0.7 all_to_all.25
  20.0 7.9 %all-to-all-start = ((bf16[32,1,24]{2,1,0:T(2,128)(2,1)}), bf16[32,1,24]{2,1,0:T(2,128)(2,1)S(1)}, u32[]{:S(2)}, u32[]{:S(2)}) async-start(bf16[32,1,24]{2,1,0:T(2,128)(2,1)} %all_to_all.25), calls=%async_computation | async-start | bytes 32768 | tf_op jit(solution)/shard_map/all_to_all | solution.py:62
  28.0 1.8 concatenate.11
  29.7 5.7 %gather_fusion.2 = bf16[768,4096]{1,0:T(8,128)(2,1)} fusion(bf16[257,4096]{1,0:T(8,128)(2,1)S(1)} %concatenate.11, s32[1024]{0:T(1024)S(1)} %get-tuple-element.21), kind=kCustom, calls=%fused_computation.2 | custom fusion | bytes 12585984 | tf_op jit(solution)/shard_map/gather | solution.py:55
  35.4 0.0 all-to-all-done
  35.4 7.4 %all-to-all-start.2 = ((bf16[32,24,4096]{2,1,0:T(8,128)(2,1)}), bf16[32,24,4096]{2,1,0:T(8,128)(2,1)}, u32[]{:S(2)}, u32[]{:S(2)}) async-start(bf16[32,24,4096]{2,1,0:T(8,128)(2,1)} %bitcast.60), calls=%async_computation.2 | async-start | bytes 12582912 | tf_op jit(solution)/shard_map/all_to_all | solution.py:60
  42.9 1.8 concatenate.10
  44.7 5.8 %gather_fusion.1 = bf16[768,4096]{1,0:T(8,128)(2,1)} fusion(bf16[257,4096]{1,0:T(8,128)(2,1)S(1)} %concatenate.10, s32[1024]{0:T(1024)S(1)} %get-tuple-element.21), kind=kCustom, calls=%fused_computation.1 | custom fusion | bytes 12585984 | tf_op jit(solution)/shard_map/gather | solution.py:56
  50.4 67.5 %all-to-all-done.2 = bf16[32,24,4096]{2,1,0:T(8,128)(2,1)} async-done(((bf16[32,24,4096]{2,1,0:T(8,128)(2,1)}), bf16[32,24,4096]{2,1,0:T(8,128)(2,1)}, u32[]{:S(2)}, u32[]{:S(2)}) %all-to-all-start.2) | async-done | bytes 6291488 | tf_op jit(solution)/shard_map/all_to_all | solution.py:60
  118.0 7.6 %all-to-all-start.1 = ((bf16[32,24,4096]{2,1,0:T(8,128)(2,1)}), bf16[32,24,4096]{2,1,0:T(8,128)(2,1)}, u32[]{:S(2)}, u32[]{:S(2)}) async-start(bf16[32,24,4096]{2,1,0:T(8,128)(2,1)} %bitcast.59), calls=%async_computation.1 | async-start | bytes 12582912 | tf_op jit(solution)/shard_map/all_to_all | solution.py:61
  125.5 0.2 reduce-scatter.8.cloned.1.call-start
  125.8 0.1 convert_reduce_fusion
  125.8 0.1 reshape.124
  125.9 0.0 copy-start
  125.9 8.8 %fusion.2 = f32[768,512]{0,1:T(8,128)} fusion(bf16[768,4096]{1,0:T(8,128)(2,1)} %bitcast.7, bf16[1,4096,512]{2,1,0:T(8,128)(2,1)} %param.11), kind=kOutput, calls=%fused_computation.12 | convolution fusion | flops 3221225472 | bytes 12058624 | tf_op jit(solution)/shard_map/dot_general | solution.py:23
  134.7 0.0 copy-done
  134.7 6.9 %fusion.5 = f32[768,512]{0,1:T(8,128)} fusion(bf16[768,4096]{1,0:T(8,128)(2,1)} %bitcast.7, bf16[1,4096,512]{2,1,0:T(8,128)(2,1)S(1)} %copy-done), kind=kOutput, calls=%fused_computation.15 | convolution fusion | flops 3221225472 | bytes 12058624 | tf_op jit(solution)/shard_map/dot_general | solution.py:24
  141.6 59.2 %all-to-all-done.1 = bf16[32,24,4096]{2,1,0:T(8,128)(2,1)} async-done(((bf16[32,24,4096]{2,1,0:T(8,128)(2,1)}), bf16[32,24,4096]{2,1,0:T(8,128)(2,1)}, u32[]{:S(2)}, u32[]{:S(2)}) %all-to-all-start.1) | async-done | bytes 6291488 | tf_op jit(solution)/shard_map/all_to_all | solution.py:61
  200.8 9.0 %fusion.9 = (bf16[768]{0:T(1024)(128)(2,1)S(1)}, bf16[768,512]{0,1:T(8,128)(2,1)S(1)}, bf16[768,512]{0,1:T(8,128)(2,1)S(1)}, bf16[768,512]{0,1:T(8,128)(2,1)S(1)}) fusion(f32[768,512]{0,1:T(8,128)} %fusion.5, f32[768,512]{0,1:T(8,128)} %fusion.2, f32[768]{0:T(1024)S(1)} %reshape.124, bf16[768,4096]{1,0:T(8,128)(2,1)} %bitcast.4, ...), kind=kOutput, calls=%fused_computation.21 | convolution fusion | flops 3228695808 | bytes 15995392 | tf_op jit(solution)/shard_map/dot_general | solution.py:8
  209.8 8.3 %convolution_bitcast_fusion = f32[1,512,4096]{2,1,0:T(8,128)} fusion(bf16[768,4096]{1,0:T(8,128)(2,1)} %bitcast.4, bf16[768,512]{0,1:T(8,128)(2,1)S(1)} %get-tuple-element.16, f32[768]{0:T(1024)S(1)} %reshape.124), kind=kOutput, calls=%fused_computation.7 | convolution fusion | flops 3222405120 | bytes 15469568 | tf_op jit(solution)/shard_map/dot_general | solution.py:8
  218.1 0.0 reduce-scatter.8.cloned.1.call-update
  218.1 0.3 reduce-scatter.4.cloned.1.call-start
  218.4 8.6 %convolution_bitcast_fusion.2 = f32[1,4096,512]{2,1,0:T(8,128)} fusion(bf16[768,4096]{1,0:T(8,128)(2,1)} %bitcast.7, bf16[768,512]{0,1:T(8,128)(2,1)S(1)} %get-tuple-element.17), kind=kOutput, calls=%fused_computation.9 | convolution fusion | flops 3221225472 | bytes 15466496 | tf_op jit(solution)/shard_map/dot_general | solution.py:8
  227.1 0.0 reduce-scatter.4.cloned.1.call-update
  227.1 0.0 reduce-scatter.6.cloned.1.call-start
  227.1 8.9 %convolution_bitcast_fusion.1 = f32[1,4096,512]{2,1,0:T(8,128)} fusion(bf16[768,4096]{1,0:T(8,128)(2,1)} %bitcast.7, bf16[768,512]{0,1:T(8,128)(2,1)S(1)} %get-tuple-element.18), kind=kOutput, calls=%fused_computation.8 | convolution fusion | flops 3221225472 | bytes 15466496 | tf_op jit(solution)/shard_map/dot_general | solution.py:8
  236.0 0.0 reduce-scatter.6.cloned.1.call-update
  236.0 0.7 convert_element_type.78
  236.8 6.5 %all-to-all-start.4 = ((bf16[32,1,24]{2,1,0:T(2,128)(2,1)}), bf16[32,1,24]{2,1,0:T(2,128)(2,1)S(1)}, u32[]{:S(2)}, u32[]{:S(2)}) async-start(bf16[32,1,24]{2,1,0:T(2,128)(2,1)} %convert_element_type.78), calls=%async_computation.4 | async-start | bytes 32768 | tf_op jit(solution)/shard_map/all_to_all | solution.py:76
  243.2 0.0 copy-start.1
  243.2 8.9 %fusion = f32[768,4096]{1,0:T(8,128)} fusion(bf16[768,512]{0,1:T(8,128)(2,1)S(1)} %get-tuple-element.17, bf16[1,4096,512]{2,1,0:T(8,128)(2,1)} %param.11), kind=kOutput, calls=%fused_computation.10 | convolution fusion | flops 3221225472 | bytes 17563648 | tf_op jit(solution)/shard_map/dot_general | solution.py:8
  252.1 0.0 copy-done.1
  252.1 8.6 %add_convert_fusion = bf16[768,4096]{1,0:T(8,128)(2,1)} fusion(f32[768,4096]{1,0:T(8,128)} %fusion, bf16[768,512]{0,1:T(8,128)(2,1)S(1)} %get-tuple-element.18, bf16[1,4096,512]{2,1,0:T(8,128)(2,1)S(1)} %copy-done.1), kind=kOutput, calls=%fused_computation.6 | convolution fusion | flops 3227516928 | bytes 23855104 | tf_op jit(solution)/shard_map/dot_general | solution.py:8
  260.7 0.0 all-to-all-done.4
  260.7 7.6 %all-to-all-start.3 = ((bf16[32,24,4096]{2,1,0:T(8,128)(2,1)}), bf16[32,24,4096]{2,1,0:T(8,128)(2,1)}, u32[]{:S(2)}, u32[]{:S(2)}) async-start(bf16[32,24,4096]{2,1,0:T(8,128)(2,1)} %bitcast.61), calls=%async_computation.3 | async-start | bytes 12582912 | tf_op jit(solution)/shard_map/all_to_all | solution.py:69
  268.3 0.1 reduce.3
  268.4 0.1 reshape.122
  268.5 3.5 gather_fusion.4
  272.0 0.2 reshape.123
  272.2 0.7 copy.25
  272.8 70.8 %all-to-all-done.3 = bf16[32,24,4096]{2,1,0:T(8,128)(2,1)} async-done(((bf16[32,24,4096]{2,1,0:T(8,128)(2,1)}), bf16[32,24,4096]{2,1,0:T(8,128)(2,1)}, u32[]{:S(2)}, u32[]{:S(2)}) %all-to-all-start.3) | async-done | bytes 6291488 | tf_op jit(solution)/shard_map/all_to_all | solution.py:69
  343.6 12.5 %gather_fusion.3 = bf16[512,4096]{1,0:T(8,128)(2,1)} fusion(bf16[768,4096]{1,0:T(8,128)(2,1)} %bitcast.11, s32[1024]{0:T(1024)S(1)} %pad_clamp_fusion), kind=kCustom, calls=%fused_computation.3 | custom fusion | bytes 8390656 | tf_op jit(solution)/shard_map/gather | solution.py:84
  356.1 7.7 %gather.21 = bf16[256,2,4096]{2,1,0:T(2,128)(2,1)} reshape(bf16[512,4096]{1,0:T(8,128)(2,1)} %gather_fusion.3) | data formatting | bytes 8388608 | tf_op jit(solution)/shard_map/gather | solution.py:84
  363.8 13.0 %reduce_sum.34 = bf16[256,4096]{1,0:T(8,128)(2,1)} reduce(bf16[256,2,4096]{2,1,0:T(2,128)(2,1)} %gather.21, bf16[]{:T(256)} %constant.34.clone.1), dimensions={1}, to_apply=%region_4.5 | reduce | flops 1048576 | bytes 6291458 | tf_op jit(solution)/shard_map/reduce_sum | solution.py:85
  376.8 0.0 reduce-scatter.8.cloned.1.call-done
  376.8 2.7 convert_element_type.76
  379.5 0.0 reduce-scatter.4.cloned.1.call-done
  379.5 2.7 convert_element_type.73
  382.2 80.0 %reduce-scatter.6.cloned.1.call-done = f32[1,1024,512]{2,1,0:T(8,128)} async-done(((f32[1,4096,512]{2,1,0:T(8,128)}), f32[1,1024,512]{2,1,0:T(8,128)}) %reduce-scatter.6.cloned.1.call-update) | async-done | bytes 2097168 | tf_op jit(solution)/shard_map/reduce_scatter | solution.py:92
  462.3 2.7 convert_element_type.74
  (9 shorter events, 0.1 us)
Async XLA Ops:
  20.0 15.4 %all-to-all-start = ((bf16[32,1,24]{2,1,0:T(2,128)(2,1)}), bf16[32,1,24]{2,1,0:T(2,128)(2,1)S(1)}, u32[]{:S(2)}, u32[]{:S(2)}) async-start(bf16[32,1,24]{2,1,0:T(2,128)(2,1)} %all_to_all.25), calls=%async_computation | async-start | bytes 32768 | tf_op jit(solution)/shard_map/all_to_all | solution.py:62
  35.4 82.5 %all-to-all-start.2 = ((bf16[32,24,4096]{2,1,0:T(8,128)(2,1)}), bf16[32,24,4096]{2,1,0:T(8,128)(2,1)}, u32[]{:S(2)}, u32[]{:S(2)}) async-start(bf16[32,24,4096]{2,1,0:T(8,128)(2,1)} %bitcast.60), calls=%async_computation.2 | async-start | bytes 12582912 | tf_op jit(solution)/shard_map/all_to_all | solution.py:60
  118.0 82.8 %all-to-all-start.1 = ((bf16[32,24,4096]{2,1,0:T(8,128)(2,1)}), bf16[32,24,4096]{2,1,0:T(8,128)(2,1)}, u32[]{:S(2)}, u32[]{:S(2)}) async-start(bf16[32,24,4096]{2,1,0:T(8,128)(2,1)} %bitcast.59), calls=%async_computation.1 | async-start | bytes 12582912 | tf_op jit(solution)/shard_map/all_to_all | solution.py:61
  125.5 251.3 %reduce-scatter.8.cloned.1.call-start = ((), (), s32[]{:S(2)}) async-start(), calls=%async_computation.10 | async-start | bytes 10485760 | tf_op jit(solution)/shard_map/reduce_scatter | solution.py:93
  125.9 8.8 %copy-start = (bf16[1,4096,512]{2,1,0:T(8,128)(2,1)S(1)}, bf16[1,4096,512]{2,1,0:T(8,128)(2,1)}, u32[]{:S(2)}) copy-start(bf16[1,4096,512]{2,1,0:T(8,128)(2,1)} %param.12) | copy-start | bytes 12582916
  218.1 161.4 %reduce-scatter.4.cloned.1.call-start = ((), (), s32[]{:S(2)}) async-start(), calls=%async_computation.8 | async-start | bytes 10485760 | tf_op jit(solution)/shard_map/reduce_scatter | solution.py:91
  227.1 235.2 %reduce-scatter.6.cloned.1.call-start = ((), (), s32[]{:S(2)}) async-start(), calls=%async_computation.9 | async-start | bytes 10485760 | tf_op jit(solution)/shard_map/reduce_scatter | solution.py:92
  236.8 23.9 %all-to-all-start.4 = ((bf16[32,1,24]{2,1,0:T(2,128)(2,1)}), bf16[32,1,24]{2,1,0:T(2,128)(2,1)S(1)}, u32[]{:S(2)}, u32[]{:S(2)}) async-start(bf16[32,1,24]{2,1,0:T(2,128)(2,1)} %convert_element_type.78), calls=%async_computation.4 | async-start | bytes 32768 | tf_op jit(solution)/shard_map/all_to_all | solution.py:76
  243.2 8.9 %copy-start.1 = (bf16[1,4096,512]{2,1,0:T(8,128)(2,1)S(1)}, bf16[1,4096,512]{2,1,0:T(8,128)(2,1)}, u32[]{:S(2)}) copy-start(bf16[1,4096,512]{2,1,0:T(8,128)(2,1)} %param.12) | copy-start | bytes 12582916
  260.7 82.9 %all-to-all-start.3 = ((bf16[32,24,4096]{2,1,0:T(8,128)(2,1)}), bf16[32,24,4096]{2,1,0:T(8,128)(2,1)}, u32[]{:S(2)}, u32[]{:S(2)}) async-start(bf16[32,24,4096]{2,1,0:T(8,128)(2,1)} %bitcast.61), calls=%async_computation.3 | async-start | bytes 12582912 | tf_op jit(solution)/shard_map/all_to_all | solution.py:69
Sparse Core Ops, SparseCore 0:
  218.3 78.3 reduce-scatter.7
  299.1 80.3 reduce-scatter.3
  381.9 80.2 reduce-scatter.5
where the time goes:
time: 476 us; the launch traced here: 471 us
  waiting for transfers between devices  278 us (58%)
  matrix products  68 us (14%)
  local copies, waits for them, and re-layouts  51.1 us (11%)
  starting transfers between devices  37.6 us (8%)
  other arithmetic  23.3 us (5%)
  between operations  14 us (3%)
    reduce_scatter x1, waiting for transfers between devices, on_device(): lax.psum_scatter(up_part, 'dp', scatter_dimension=1, tiled=True)  80 us
    all_to_all x1, waiting for transfers between devices, on_device(): lax.all_to_all(pick_grad.reshape(experts, capacity, width), 'expert', spl...  70.8 us
    all_to_all x1, waiting for transfers between devices, on_device(): lax.all_to_all(send_x, 'expert', split_axis=0, concat_axis=0, tiled=True)  67.5 us
    all_to_all x1, waiting for transfers between devices, on_device(): lax.all_to_all(send_dy, 'expert', split_axis=0, concat_axis=0, tiled=True)  59.2 us
    dot_general x6, matrix products, contract(): lax.dot_general(left, right, (((left_dim,), (right_dim,)), ((), ())), pre...  52.3 us
    gather x2, local copies, waits for them, and re-layouts, on_device(): back_rows.reshape(-1, width)[places].astype(jnp.float32)  20.2 us
    reduce_sum x1, other arithmetic, on_device(): grad_tokens = jnp.sum(pairs, axis=1).astype(jnp.bfloat16)  13 us
  transfers between devices with their start and end apart: 8, of which 4 were waited for; matrix products, arithmetic and copies ran while one was open for 23% of the time, Pallas kernels for 0%

commit v1 on v0

v1 whole, which is shorter than its diff:
```python
import functools

import jax
import jax.numpy as jnp
from jax import lax
from jax.experimental import pallas as pl
from jax.experimental.pallas import tpu as pltpu
from jax.sharding import PartitionSpec as P

MESH = pl.DeviceIdType.MESH
NX, NY, NZ, NE = 4, 4, 4, 32
CAP = 24
D, HID = 4096, 512
SLICE = D // NZ
GROUP = 8
GROUPS = NE // GROUP
ROWS = GROUP * CAP
OFFSETS = (
    (1, 0), (3, 0), (0, 1), (0, 3), (1, 1), (3, 3), (1, 3), (3, 1),
    (2, 0), (0, 2), (1, 2), (3, 2), (2, 1), (2, 3), (2, 2),
)


def offset(i, core):
    dx, dy = OFFSETS[i]
    return dx + core * (dy - dx), dy + core * (dx - dy)


def expert_at(x, y, core):
    return (y % NY) * (2 * NX) + (x % NX) * 2 + core


def nt(left, right):
    return lax.dot_general(left, right, (((1,), (1,)), ((), ())), preferred_element_type=jnp.float32)


def tn(left, right):
    return lax.dot_general(left, right, (((0,), (0,)), ((), ())), preferred_element_type=jnp.float32)


def kernel(
    sx, sdy, wg_h, wu_h, wd_h,
    back, back_c, out_g, out_u, out_d,
    xr, dyr, pg, pc, wg, wu, wd, xz, gz, gown, hid, dn_out, dn_in, fa, fb,
    w_sem, loc_sem, x_recv, dy_recv, x_send, dy_send, pg_recv, pg_send, pc_recv, pc_send,
    xz_recv, xz_send, gz_recv, gz_send, dn_recv, dn_send,
):
    z = lax.axis_index("dp")
    ex = lax.axis_index("expert")
    c = ex % 2
    x = (ex // 2) % NX
    y = ex // (2 * NX)

    loads = [
        pltpu.make_async_copy(wg_h, wg, w_sem.at[0]),
        pltpu.make_async_copy(wu_h, wu, w_sem.at[1]),
        pltpu.make_async_copy(wd_h, wd, w_sem.at[2]),
        pltpu.make_async_copy(sx.at[ex], xr.at[0], loc_sem.at[0]),
        pltpu.make_async_copy(sdy.at[ex], dyr.at[0], loc_sem.at[1]),
    ]

    barrier = pltpu.get_barrier_semaphore()

    def greet(k, carry):
        pl.semaphore_signal(barrier, inc=1, device_id=(z, (ex + k) % NE), device_id_type=MESH)
        return carry

    lax.fori_loop(1, NE, greet, 0)
    for j in range(1, NZ):
        pl.semaphore_signal(barrier, inc=1, device_id=((z + j) % NZ, ex), device_id_type=MESH)
    for load in loads:
        load.start()
    pl.semaphore_wait(barrier, NE - 1 + NZ - 1)

    def to_expert(src, dst, send, recv, i, core):
        if i < 0:
            to, slot = ex + 1 - 2 * c, 1
            group = 0
        else:
            dx, dy = offset(i, c)
            to, slot = expert_at(x + dx, y + dy, core), 2 + 2 * i + c
            group = (2 + 2 * i) // GROUP
        return pltpu.make_async_remote_copy(
            src_ref=src.at[to], dst_ref=dst.at[slot], send_sem=send, recv_sem=recv.at[group],
            device_id=(z, to), device_id_type=MESH,
        )

    for g in range(GROUPS):
        for src, dst, send, recv in ((sx, xr, x_send, x_recv), (sdy, dyr, dy_send, dy_recv)):
            for slot in range(GROUP * g, GROUP * (g + 1), 2):
                if slot == 0:
                    to_expert(src, dst, send, recv, -1, 0).start()
                else:
                    for core in range(2):
                        to_expert(src, dst, send, recv, (slot - 2) // 2, core).start()

    def wait_recv(dst, sem):
        pltpu.make_async_remote_copy(
            src_ref=dst, dst_ref=dst, send_sem=x_send, recv_sem=sem,
            device_id=(z, (ex + 1) % NE), device_id_type=MESH,
        ).wait_recv()

    def wait_send(src, sem):
        pltpu.make_async_remote_copy(
            src_ref=src, dst_ref=src, send_sem=sem, recv_sem=x_recv.at[0],
            device_id=(z, (ex + 1) % NE), device_id_type=MESH,
        ).wait_send()

    def arrive(dst, recv, own, g):
        @pl.when(g == 0)
        def _():
            loads[own].wait()
            wait_recv(dst.at[pl.ds(1, GROUP - 1)], recv.at[0])

        @pl.when(g > 0)
        def _():
            wait_recv(dst.at[pl.ds(GROUP * g, GROUP)], recv.at[g])

    def over_z(src, dst, send, recv, j):
        return pltpu.make_async_remote_copy(
            src_ref=src, dst_ref=dst, send_sem=send, recv_sem=recv,
            device_id=((z + j) % NZ, ex), device_id_type=MESH,
        )

    def give_back(slot):
        if slot == 0:
            return [
                pltpu.make_async_copy(pg.at[0], back.at[ex], loc_sem.at[2]),
                pltpu.make_async_copy(pc.at[0], back_c.at[ex], loc_sem.at[3]),
            ]
        if slot == 1:
            to = ex + 1 - 2 * c
        else:
            i, core = (slot - 2) // 2, slot % 2
            dx, dy = offset(i, core)
            to = expert_at(x - dx, y - dy, core)
        return [
            pltpu.make_async_remote_copy(
                src_ref=src.at[slot], dst_ref=dst.at[ex], send_sem=send, recv_sem=recv,
                device_id=(z, to), device_id_type=MESH,
            )
            for src, dst, send, recv in ((pg, back, pg_send, pg_recv), (pc, back_c, pc_send, pc_recv))
        ]

    for load in loads[:3]:
        load.wait()

    KC = 1024

    def group_step(g, carry):
        base = pl.multiple_of(GROUP * g, GROUP)
        rows = pl.ds(pl.multiple_of(g * ROWS, ROWS), ROWS)
        arrive(xr, x_recv, 3, g)
        for j in (2, 1, 3):
            cols = pl.ds(pl.multiple_of((z + j) % NZ * SLICE, SLICE), SLICE)
            over_z(xr.at[pl.ds(base, GROUP), :, cols], xz.at[j - 1, pl.ds(base, GROUP)], xz_send, xz_recv, j).start()

        fa[...] = jnp.zeros_like(fa)
        fb[...] = jnp.zeros_like(fb)

        def forward(k, cc):
            kk = pl.ds(pl.multiple_of(k * KC, KC), KC)
            xk = xr[pl.ds(base, GROUP), :, kk].reshape(ROWS, KC)
            fa[...] += jnp.dot(xk, wg[kk, :], preferred_element_type=jnp.float32)
            fb[...] += jnp.dot(xk, wu[kk, :], preferred_element_type=jnp.float32)
            return cc

        lax.fori_loop(0, D // KC, forward, 0)
        gate = fa[...]
        upper = fb[...]
        sigma = 1.0 / (1.0 + jnp.exp(-gate))
        swish = gate * sigma
        hidden = (swish * upper).astype(jnp.bfloat16)
        hid[rows, :] = hidden
        fa[...] = upper * sigma * (1.0 + gate * (1.0 - sigma))
        fb[...] = swish

        arrive(dyr, dy_recv, 4, g)

        @pl.when(g == GROUPS - 1)
        def _():
            for slot in range(NE - GROUP):
                for copy in give_back(slot):
                    copy.start()

        def backward(k, hg):
            kk = pl.ds(pl.multiple_of(k * KC, KC), KC)
            dk = dyr[pl.ds(base, GROUP), :, kk].reshape(ROWS, KC)
            return hg + nt(dk, wd[:, kk])

        hg = lax.fori_loop(0, D // KC, backward, jnp.zeros((ROWS, HID), jnp.float32))
        gown[rows, pl.ds(0, HID)] = (hg * fa[...]).astype(jnp.bfloat16)
        gown[rows, pl.ds(HID, HID)] = (hg * fb[...]).astype(jnp.bfloat16)
        for j in (2, 1, 3):
            over_z(gown.at[rows], gz.at[j - 1, rows], gz_send, gz_recv, j).start()
        total = jnp.sum(hid[rows, :].astype(jnp.float32) * hg, axis=1, keepdims=True)
        total = jnp.broadcast_to(total, (ROWS, 128))
        high = total.astype(jnp.bfloat16).astype(jnp.float32)
        lane = lax.broadcasted_iota(jnp.int32, (ROWS, 128), 1)
        pc[pl.ds(base, GROUP)] = (
            jnp.where(lane < 64, high, total - high).astype(jnp.bfloat16).reshape(GROUP, CAP, 128)
        )

        def inward(k, cc):
            kk = pl.ds(pl.multiple_of(k * KC, KC), KC)
            part = nt(gown[rows, pl.ds(0, HID)], wg[kk, :]) + nt(gown[rows, pl.ds(HID, HID)], wu[kk, :])
            pg[pl.ds(base, GROUP), :, kk] = part.astype(jnp.bfloat16).reshape(GROUP, CAP, KC)
            return cc

        lax.fori_loop(0, D // KC, inward, 0)
        return carry

    lax.fori_loop(0, GROUPS, group_step, 0)
    for slot in range(NE - GROUP, NE):
        for copy in give_back(slot):
            copy.start()

    def down_part(j):
        cols = pl.ds(pl.multiple_of((z + j) % NZ * SLICE, SLICE), SLICE)
        total = jnp.zeros((HID, SLICE), jnp.float32)

        def add(g, total):
            rows = pl.ds(pl.multiple_of(g * ROWS, ROWS), ROWS)
            dk = dyr[pl.ds(pl.multiple_of(GROUP * g, GROUP), GROUP), :, cols].reshape(ROWS, SLICE)
            return total + tn(hid[rows, :], dk)

        return lax.fori_loop(0, GROUPS, add, total)

    for j in (2, 1, 3):
        dn_out[j - 1] = down_part(j).astype(jnp.bfloat16)
        over_z(dn_out.at[j - 1], dn_in.at[j - 1], dn_send, dn_recv, j).start()

    wait_recv(xz, xz_recv)
    wait_recv(gz, gz_recv)
    CB = 256

    def wide(k, carry):
        off = pl.multiple_of(k * CB, CB)
        mine = pl.ds(pl.multiple_of(z * SLICE + off, CB), CB)
        total = tn(xr[:, :, mine].reshape(NE * CAP, CB), gown[...])
        for j in range(NZ - 1):
            total += tn(xz[j, :, :, pl.ds(off, CB)].reshape(NE * CAP, CB), gz[j])
        out_g[pl.ds(off, CB), :] = total[:, :HID].astype(jnp.bfloat16)
        out_u[pl.ds(off, CB), :] = total[:, HID:].astype(jnp.bfloat16)
        return carry

    lax.fori_loop(0, SLICE // CB, wide, 0)

    wait_recv(dn_in, dn_recv)
    own = down_part(0)
    for j in range(NZ - 1):
        own += dn_in[j].astype(jnp.float32)
    out_d[...] = own.astype(jnp.bfloat16)

    most = pl.ds(0, NE - 1)
    wait_send(sx.at[most], x_send)
    wait_send(sdy.at[most], dy_send)
    wait_send(xz, xz_send)
    wait_send(gz, gz_send)
    wait_send(dn_out, dn_send)
    wait_send(pg.at[most], pg_send)
    wait_send(pc.at[most], pc_send)
    for copy in give_back(0):
        copy.wait()
    wait_recv(back.at[most], pg_recv)
    wait_recv(back_c.at[most], pc_recv)


def exchange(send_x, send_dy, w_gate, w_up, w_down):
    bf = jnp.bfloat16
    any_ = pl.BlockSpec(memory_space=pl.ANY)
    vm = pl.BlockSpec(memory_space=pltpu.VMEM)
    dma = pltpu.SemaphoreType.DMA
    return pl.pallas_call(
        kernel,
        out_shape=(
            jax.ShapeDtypeStruct((NE, CAP, D), bf),
            jax.ShapeDtypeStruct((NE, CAP, 128), bf),
            jax.ShapeDtypeStruct((SLICE, HID), bf),
            jax.ShapeDtypeStruct((SLICE, HID), bf),
            jax.ShapeDtypeStruct((HID, SLICE), bf),
        ),
        in_specs=[any_] * 5,
        out_specs=(any_, any_, vm, vm, vm),
        scratch_shapes=[
            pltpu.VMEM((NE, CAP, D), bf),
            pltpu.VMEM((NE, CAP, D), bf),
            pltpu.VMEM((NE, CAP, D), bf),
            pltpu.VMEM((NE, CAP, 128), bf),
            pltpu.VMEM((D, HID), bf),
            pltpu.VMEM((D, HID), bf),
            pltpu.VMEM((HID, D), bf),
            pltpu.VMEM((NZ - 1, NE, CAP, SLICE), bf),
            pltpu.VMEM((NZ - 1, NE * CAP, 2 * HID), bf),
            pltpu.VMEM((NE * CAP, 2 * HID), bf),
            pltpu.VMEM((NE * CAP, HID), bf),
            pltpu.VMEM((NZ - 1, HID, SLICE), bf),
            pltpu.VMEM((NZ - 1, HID, SLICE), bf),
            pltpu.VMEM((ROWS, HID), jnp.float32),
            pltpu.VMEM((ROWS, HID), jnp.float32),
            dma((3,)), dma((4,)), dma((GROUPS,)), dma((GROUPS,)),
        ] + [dma] * 12,
        compiler_params=pltpu.CompilerParams(
            collective_id=0, has_side_effects=True, vmem_limit_bytes=63 * 2**20
        ),
    )(send_x, send_dy, w_gate, w_up, w_down)


def on_device(tokens, grad_out, expert_ids, combine, w_gate, w_up, w_down):
    bf = jnp.bfloat16
    rows = tokens.shape[0]
    labels = jnp.arange(NE, dtype=jnp.int32)
    hits = [(expert_ids[:, k, None] == labels[None, :]).astype(bf) for k in range(2)]
    order = jnp.arange(rows, dtype=jnp.int32)
    before = (order[None, :] < order[:, None]).astype(bf)
    earlier = jnp.dot(before, hits[0] + hits[1], preferred_element_type=jnp.float32)
    places = [
        expert_ids[:, k] * CAP + jnp.sum(earlier * hits[k].astype(jnp.float32), axis=1).astype(jnp.int32)
        for k in range(2)
    ]
    slots = jnp.arange(NE * CAP, dtype=jnp.int32)
    put = [(slots[:, None] == places[k][None, :]).astype(bf) for k in range(2)]
    put_x = put[0] + put[1]
    put_dy = put[0] * combine[:, 0][None, :] + put[1] * combine[:, 1][None, :]
    send_x = jnp.dot(put_x, tokens, preferred_element_type=jnp.float32).astype(bf)
    send_dy = jnp.dot(put_dy, grad_out, preferred_element_type=jnp.float32).astype(bf)
    back, back_c, grad_gate, grad_up, grad_down = exchange(
        send_x.reshape(NE, CAP, D), send_dy.reshape(NE, CAP, D), w_gate[0], w_up[0], w_down[0]
    )
    grad_tokens = lax.dot_general(
        put_x, back.reshape(NE * CAP, D), (((0,), (0,)), ((), ())), preferred_element_type=jnp.float32
    ).astype(bf)
    sums = back_c.reshape(NE * CAP, 128)
    parts = [
        lax.dot_general(put[k], sums, (((0,), (0,)), ((), ())), preferred_element_type=jnp.float32)
        for k in range(2)
    ]
    grad_combine = jnp.stack([p[:, 0] + p[:, 64] for p in parts], axis=1) / combine.astype(jnp.float32)
    return grad_tokens, grad_combine.astype(bf), grad_gate[None], grad_up[None], grad_down[None]


def solution(mesh):
    return jax.shard_map(
        on_device,
        mesh=mesh,
        in_specs=(
            P(("dp", "expert"), None),
            P(("dp", "expert"), None),
            P(("dp", "expert"), None),
            P(("dp", "expert"), None),
            P("expert", None, None),
            P("expert", None, None),
            P("expert", None, None),
        ),
        out_specs=(
            P(("dp", "expert"), None),
            P(("dp", "expert"), None),
            P("expert", "dp", None),
            P("expert", "dp", None),
            P("expert", None, "dp"),
        ),
        check_vma=False,
    )
```

time: 476 us -> 278 us (0.58)
  the two profiles are of different devices: /device:TPU:67 before, /device:TPU:123 now
where the time goes in v1:
time: 278 us; the launch traced here: 277 us
  Pallas kernels  254 us (91%)
  matrix products  17.6 us (6%)
  local copies, waits for them, and re-layouts  4.47 us (2%)
    pallas_call x1, Pallas kernels, exchange(): pl.pallas_call(kernel, out_shape=(jax.ShapeDtypeStruct((NE, CAP, D), bf),...  254 us
    dot_general x1, matrix products, on_device(): jnp.dot(put_dy, grad_out, preferred_element_type=jnp.float32).astype(bf)  6.21 us
    dot_general x1, matrix products, on_device(): lax.dot_general(put_x, back.reshape(NE * CAP, D), (((0,), (0,)), ((), ())...  6.15 us

profile of v1, /device:TPU:123, one launch (start us, length us, event | category | flops | bytes accessed | tf_op | source)
XLA Modules:
  0.0 277.4 jit_solution(9892463505127141751)
XLA Ops:
  0.6 0.8 slice_reduce_fusion.1
  1.4 0.8 fusion.32
  2.2 0.2 multiply_reduce_fusion.1
  2.4 0.0 copy-start
  2.4 6.2 %convolution_convert_fusion = bf16[768,4096]{1,0:T(8,128)(2,1)} fusion(bf16[256,4096]{1,0:T(8,128)(2,1)} %param.8, s32[256]{0:T(256)S(1)} %get-tuple-element.21, s32[256]{0:T(256)S(1)} %get-tuple-element.22, bf16[256]{0:T(256)(128)(2,1)S(1)} %get-tuple-element.18, bf16[256]{0:T(256)(128)(2,1)S(1)} %get-tuple-element.17), kind=kOutput, calls=%fused_computation | convolution fusion | flops 1615331328 | bytes 8391680 | tf_op jit(solution)/shard_map/dot_general | solution.py:326
  8.6 0.0 copy-done
  8.6 4.5 %convolution_convert_fusion.1 = bf16[768,4096]{1,0:T(8,128)(2,1)} fusion(bf16[256,4096]{1,0:T(8,128)(2,1)S(1)} %copy-done, s32[256]{0:T(256)S(1)} %get-tuple-element.21, s32[256]{0:T(256)S(1)} %get-tuple-element.22), kind=kOutput, calls=%fused_computation.1 | convolution fusion | flops 1615331328 | bytes 8390656 | tf_op jit(solution)/shard_map/dot_general | solution.py:325
  13.1 253.9 %shard_map.110 = (bf16[32,24,4096]{2,1,0:T(8,128)(2,1)}, bf16[32,24,128]{2,1,0:T(8,128)(2,1)}, bf16[1024,512]{1,0:T(8,128)(2,1)}, bf16[1024,512]{1,0:T(8,128)(2,1)}, bf16[512,1024]{1,0:T(8,128)(2,1)}) custom-call(bf16[32,24,4096]{2,1,0:T(8,128)(2,1)} %bitcast.18, bf16[32,24,4096]{2,1,0:T(8,128)(2,1)} %bitcast.17, bf16[4096,512]{1,0:T(8,128)(2,1)} %bitcast.20, ...), custom_call_target="tpu_custom_call" | custom-call | tf_op jit(solution)/shard_map/pallas_call | solution.py:274
  267.0 0.0 copy-start.5
  267.0 0.0 copy-start.4
  267.1 0.0 copy-start.3
  267.1 0.0 copy-start.2
  267.1 6.2 %convolution_convert_fusion.2 = bf16[256,4096]{1,0:T(8,128)(2,1)} fusion(bf16[768,4096]{1,0:T(8,128)(2,1)} %bitcast.19, s32[256]{0:T(256)S(1)} %get-tuple-element.21, s32[256]{0:T(256)S(1)} %get-tuple-element.22), kind=kOutput, calls=%fused_computation.2 | convolution fusion | flops 1613234176 | bytes 8390656 | tf_op jit(solution)/shard_map/dot_general | solution.py:330
  273.2 0.0 copy-done.5
  273.2 0.0 copy-start.1
  273.2 0.3 fusion.3
  273.6 0.3 fusion
  273.9 0.0 copy-done.4
  273.9 0.6 fusion.30
  274.5 0.0 copy-done.3
  274.5 1.0 copy.15
  275.4 0.0 copy-done.2
  275.4 1.0 copy.16
  276.4 0.0 copy-done.1
  276.4 1.0 copy.17
  (3 shorter events, 0.0 us)
Async XLA Ops:
  2.4 6.2 %copy-start = (bf16[256,4096]{1,0:T(8,128)(2,1)S(1)}, bf16[256,4096]{1,0:T(8,128)(2,1)}, u32[]{:S(2)}) copy-start(bf16[256,4096]{1,0:T(8,128)(2,1)} %param.7) | copy-start | bytes 6291460
  267.0 6.2 %copy-start.5 = (bf16[32,24,128]{2,1,0:T(8,128)(2,1)S(1)}, bf16[32,24,128]{2,1,0:T(8,128)(2,1)}, u32[]{:S(2)}) copy-start(bf16[32,24,128]{2,1,0:T(8,128)(2,1)} %get-tuple-element.11) | copy-start | bytes 589828
  267.0 6.8 %copy-start.4 = (bf16[256,2]{0,1:T(2,128)(2,1)S(1)}, bf16[256,2]{0,1:T(2,128)(2,1)}, u32[]{:S(2)}) copy-start(bf16[256,2]{0,1:T(2,128)(2,1)} %param.10) | copy-start | bytes 3076
  267.1 7.4 %copy-start.3 = (bf16[1024,512]{1,0:T(8,128)(2,1)S(1)}, bf16[1024,512]{1,0:T(8,128)(2,1)}, u32[]{:S(2)}) copy-start(bf16[1024,512]{1,0:T(8,128)(2,1)} %get-tuple-element.12) | copy-start | bytes 3145732
  267.1 8.4 %copy-start.2 = (bf16[1024,512]{1,0:T(8,128)(2,1)S(1)}, bf16[1024,512]{1,0:T(8,128)(2,1)}, u32[]{:S(2)}) copy-start(bf16[1024,512]{1,0:T(8,128)(2,1)} %get-tuple-element.13) | copy-start | bytes 3145732
  273.2 3.2 %copy-start.1 = (bf16[512,1024]{1,0:T(8,128)(2,1)S(1)}, bf16[512,1024]{1,0:T(8,128)(2,1)}, u32[]{:S(2)}) copy-start(bf16[512,1024]{1,0:T(8,128)(2,1)} %get-tuple-element.14) | copy-start | bytes 3145732

commit v2 on v1

--- a/solution.py
+++ b/solution.py
@@ -1,5 +1,3 @@
-import functools
-
 import jax
 import jax.numpy as jnp
 from jax import lax
@@ -15,6 +13,10 @@
 GROUP = 8
 GROUPS = NE // GROUP
 ROWS = GROUP * CAP
+TOK = 256
+SC = 512
+VMEM_BYTES = 63 * 2**20
+RETURNS = {2: range(0, 8), 3: range(8, 24)}
 OFFSETS = (
     (1, 0), (3, 0), (0, 1), (0, 3), (1, 1), (3, 3), (1, 3), (3, 1),
     (2, 0), (0, 2), (1, 2), (3, 2), (2, 1), (2, 3), (2, 2),
@@ -39,12 +41,13 @@
 
 
 def kernel(
-    sx, sdy, wg_h, wu_h, wd_h,
-    back, back_c, out_g, out_u, out_d,
-    xr, dyr, pg, pc, wg, wu, wd, xz, gz, gown, hid, dn_out, dn_in, fa, fb,
-    w_sem, loc_sem, x_recv, dy_recv, x_send, dy_send, pg_recv, pg_send, pc_recv, pc_send,
-    xz_recv, xz_send, gz_recv, gz_send, dn_recv, dn_send,
+    ids_t, weight_t, tok_h, dy_h, wg_h, wu_h, wd_h,
+    back, sx, sdy, put_t, out_c, wide_h, down_h,
+    tokdy, stage, out_gu, out_d, put, put0, put1, put_dy, back_c, xr, dyr, pg, pc, wg, wu, wd, xz, gz, gown, hid, dn_in, dn_rel, fa, fb,
+    in_sem, out_sem, st_sem, w_sem, loc_sem, x_recv, dy_recv, x_send, dy_send, pg_recv, pg_send, pc_recv, pc_send,
+    xz_recv, xz_send, gz_next, gz_prev, gz_far, gz_send, dn_recv, rel_recv, dn_send,
 ):
+    bf, f32 = jnp.bfloat16, jnp.float32
     z = lax.axis_index("dp")
     ex = lax.axis_index("expert")
     c = ex % 2
@@ -68,9 +71,46 @@
     lax.fori_loop(1, NE, greet, 0)
     for j in range(1, NZ):
         pl.semaphore_signal(barrier, inc=1, device_id=((z + j) % NZ, ex), device_id_type=MESH)
-    for load in loads:
+    fetch = [pltpu.make_async_copy(tok_h, tokdy.at[0], in_sem.at[0]), pltpu.make_async_copy(dy_h, tokdy.at[1], in_sem.at[1])]
+    for load in fetch + loads[:3]:
         load.start()
-    pl.semaphore_wait(barrier, NE - 1 + NZ - 1)
+
+    ids = [ids_t[k : k + 1, :].astype(f32) for k in range(2)]
+    weight = weight_t[...].astype(f32)
+    label = lax.broadcasted_iota(jnp.int32, (NE, TOK), 0).astype(f32)
+    hits = [(label == ids[k]).astype(f32) for k in range(2)]
+    first = lax.broadcasted_iota(jnp.int32, (TOK, TOK), 0)
+    second = lax.broadcasted_iota(jnp.int32, (TOK, TOK), 1)
+    before = (first < second).astype(f32).astype(bf)
+    earlier = jnp.dot((hits[0] + hits[1]).astype(bf), before, preferred_element_type=f32)
+    places = [ids[k] * CAP + jnp.sum(earlier * hits[k], axis=0, keepdims=True) for k in range(2)]
+    index = lax.broadcasted_iota(jnp.int32, (NE * CAP, TOK), 0).astype(f32)
+    put_k = [(index == places[k]).astype(f32) for k in range(2)]
+    put[...] = (put_k[0] + put_k[1]).astype(bf)
+    put0[...] = put_k[0].astype(bf)
+    put1[...] = put_k[1].astype(bf)
+    put_dy[...] = (put_k[0] * weight[0:1] + put_k[1] * weight[1:2]).astype(bf)
+
+    def lay_out(which, rows, dst):
+        def block(k, carry):
+            kk = pl.ds(pl.multiple_of(k * SC, SC), SC)
+            half = k % 2
+            move = pltpu.make_async_copy(stage.at[half], dst.at[:, :, kk], st_sem.at[half])
+
+            @pl.when(k >= 2)
+            def _():
+                move.wait()
+
+            made = jnp.dot(rows[...], tokdy[which, :, kk], preferred_element_type=f32)
+            stage[half] = made.astype(bf).reshape(NE, CAP, SC)
+            move.start()
+            return carry
+
+        fetch[which].wait()
+        lax.fori_loop(0, D // SC, block, 0)
+        for half in range(2):
+            pltpu.make_async_copy(stage.at[half], dst.at[:, :, pl.ds(0, SC)], st_sem.at[half]).wait()
+        loads[3 + which].start()
 
     def to_expert(src, dst, send, recv, i, core):
         if i < 0:
@@ -85,8 +125,12 @@
             device_id=(z, to), device_id_type=MESH,
         )
 
+    lay_out(0, put, sx)
+    pl.semaphore_wait(barrier, NE - 1 + NZ - 1)
     for g in range(GROUPS):
         for src, dst, send, recv in ((sx, xr, x_send, x_recv), (sdy, dyr, dy_send, dy_recv)):
+            if g == 0 and src is sdy:
+                lay_out(1, put_dy, sdy)
             for slot in range(GROUP * g, GROUP * (g + 1), 2):
                 if slot == 0:
                     to_expert(src, dst, send, recv, -1, 0).start()
@@ -142,8 +186,21 @@
             for src, dst, send, recv in ((pg, back, pg_send, pg_recv), (pc, back_c, pc_send, pc_recv))
         ]
 
+    for k in range(NE * CAP // TOK):
+        part = pl.ds(k * TOK, TOK)
+        put_t[:, part] = put[part, :].astype(f32).T.astype(bf)
+
     for load in loads[:3]:
         load.wait()
+
+    def pass_on(g):
+        rows = pl.ds(pl.multiple_of(g * ROWS, ROWS), ROWS)
+        wait_recv(gz.at[0, rows], gz_next.at[g])
+        low = pl.ds(pl.multiple_of(g * ROWS, ROWS // 2), ROWS // 2)
+        over_z(gz.at[0, low], gz.at[1, low], gz_send, gz_far, 1).start()
+        wait_recv(gz.at[2, rows], gz_prev.at[g])
+        high = pl.ds(pl.multiple_of(g * ROWS + ROWS // 2, ROWS // 2), ROWS // 2)
+        over_z(gz.at[2, high], gz.at[1, high], gz_send, gz_far, 3).start()
 
     KC = 1024
 
@@ -175,13 +232,19 @@
         fa[...] = upper * sigma * (1.0 + gate * (1.0 - sigma))
         fb[...] = swish
 
+        @pl.when(g >= 1)
+        def _():
+            pass_on(g - 1)
+
         arrive(dyr, dy_recv, 4, g)
 
-        @pl.when(g == GROUPS - 1)
-        def _():
-            for slot in range(NE - GROUP):
-                for copy in give_back(slot):
-                    copy.start()
+        for step, slots in RETURNS.items():
+
+            @pl.when(g == step)
+            def _():
+                for slot in slots:
+                    for copy in give_back(slot):
+                        copy.start()
 
         def backward(k, hg):
             kk = pl.ds(pl.multiple_of(k * KC, KC), KC)
@@ -191,8 +254,8 @@
         hg = lax.fori_loop(0, D // KC, backward, jnp.zeros((ROWS, HID), jnp.float32))
         gown[rows, pl.ds(0, HID)] = (hg * fa[...]).astype(jnp.bfloat16)
         gown[rows, pl.ds(HID, HID)] = (hg * fb[...]).astype(jnp.bfloat16)
-        for j in (2, 1, 3):
-            over_z(gown.at[rows], gz.at[j - 1, rows], gz_send, gz_recv, j).start()
+        over_z(gown.at[rows], gz.at[0, rows], gz_send, gz_next.at[g], 1).start()
+        over_z(gown.at[rows], gz.at[2, rows], gz_send, gz_prev.at[g], 3).start()
         total = jnp.sum(hid[rows, :].astype(jnp.float32) * hg, axis=1, keepdims=True)
         total = jnp.broadcast_to(total, (ROWS, 128))
         high = total.astype(jnp.bfloat16).astype(jnp.float32)
@@ -215,6 +278,8 @@
         for copy in give_back(slot):
             copy.start()
 
+    pass_on(GROUPS - 1)
+
     def down_part(j):
         cols = pl.ds(pl.multiple_of((z + j) % NZ * SLICE, SLICE), SLICE)
         total = jnp.zeros((HID, SLICE), jnp.float32)
@@ -226,12 +291,27 @@
 
         return lax.fori_loop(0, GROUPS, add, total)
 
-    for j in (2, 1, 3):
-        dn_out[j - 1] = down_part(j).astype(jnp.bfloat16)
-        over_z(dn_out.at[j - 1], dn_in.at[j - 1], dn_send, dn_recv, j).start()
+    half = HID // 2
+    low, high = pl.ds(0, half), pl.ds(half, half)
+
+    def dn_out(h, j):
+        return tokdy.at[h, :, pl.ds((j - 1) * SLICE, SLICE)]
+
+    def make_down(j):
+        part = down_part(j).astype(bf)
+        dn_out(0, j)[...] = part[:half]
+        dn_out(1, j)[...] = part[half:]
+
+    make_down(2)
+    over_z(dn_out(0, 2), dn_rel.at[0], dn_send, rel_recv.at[0], 1).start()
+    over_z(dn_out(1, 2), dn_rel.at[1], dn_send, rel_recv.at[1], 3).start()
+    make_down(1)
+    over_z(dn_out(1, 1), dn_in.at[0, high], dn_send, dn_recv, 1).start()
+    make_down(3)
+    over_z(dn_out(0, 3), dn_in.at[1, low], dn_send, dn_recv, 3).start()
 
     wait_recv(xz, xz_recv)
-    wait_recv(gz, gz_recv)
+    wait_recv(gz.at[1], gz_far)
     CB = 256
 
     def wide(k, carry):
@@ -240,34 +320,51 @@
         total = tn(xr[:, :, mine].reshape(NE * CAP, CB), gown[...])
         for j in range(NZ - 1):
             total += tn(xz[j, :, :, pl.ds(off, CB)].reshape(NE * CAP, CB), gz[j])
-        out_g[pl.ds(off, CB), :] = total[:, :HID].astype(jnp.bfloat16)
-        out_u[pl.ds(off, CB), :] = total[:, HID:].astype(jnp.bfloat16)
+        out_gu[pl.ds(off, CB), :] = total.astype(bf)
         return carry
 
     lax.fori_loop(0, SLICE // CB, wide, 0)
-
+    wide_out = pltpu.make_async_copy(out_gu, wide_h, out_sem.at[0])
+    wide_out.start()
+
+    for h, j in ((0, 1), (1, 3)):
+        wait_recv(dn_rel.at[h], rel_recv.at[h])
+        dn_out(h, j)[...] = (dn_out(h, j)[...].astype(f32) + dn_rel[h].astype(f32)).astype(bf)
+        over_z(dn_out(h, j), dn_in.at[h, high if h else low], dn_send, dn_recv, j).start()
+    own = down_part(0)
     wait_recv(dn_in, dn_recv)
-    own = down_part(0)
-    for j in range(NZ - 1):
-        own += dn_in[j].astype(jnp.float32)
-    out_d[...] = own.astype(jnp.bfloat16)
+    for j in range(2):
+        own += dn_in[j].astype(f32)
+    out_d[...] = own.astype(bf)
+    down_out = pltpu.make_async_copy(out_d, down_h, out_sem.at[1])
+    down_out.start()
 
     most = pl.ds(0, NE - 1)
     wait_send(sx.at[most], x_send)
     wait_send(sdy.at[most], dy_send)
     wait_send(xz, xz_send)
     wait_send(gz, gz_send)
-    wait_send(dn_out, dn_send)
+    wait_send(tokdy.at[:, :, pl.ds(0, (NZ - 1) * SLICE)], dn_send)
     wait_send(pg.at[most], pg_send)
     wait_send(pc.at[most], pc_send)
     for copy in give_back(0):
         copy.wait()
+    wait_recv(back_c.at[most], pc_recv)
+    sums = back_c[...].reshape(NE * CAP, 128)
+    both = [tn(rows[...], sums) for rows in (put0, put1)]
+    lane = lax.broadcasted_iota(jnp.int32, (TOK, 128), 1)
+    out_c[...] = jnp.where(
+        lane == 0,
+        jnp.sum(jnp.where(lane % 64 == 0, both[0], 0.0), axis=1, keepdims=True),
+        jnp.sum(jnp.where(lane % 64 == 0, both[1], 0.0), axis=1, keepdims=True),
+    )
     wait_recv(back.at[most], pg_recv)
-    wait_recv(back_c.at[most], pc_recv)
-
-
-def exchange(send_x, send_dy, w_gate, w_up, w_down):
-    bf = jnp.bfloat16
+    wide_out.wait()
+    down_out.wait()
+
+
+def exchange(ids_t, weight_t, tokens, grad_out, w_gate, w_up, w_down):
+    bf, f32 = jnp.bfloat16, jnp.float32
     any_ = pl.BlockSpec(memory_space=pl.ANY)
     vm = pl.BlockSpec(memory_space=pltpu.VMEM)
     dma = pltpu.SemaphoreType.DMA
@@ -275,14 +372,25 @@
         kernel,
         out_shape=(
             jax.ShapeDtypeStruct((NE, CAP, D), bf),
-            jax.ShapeDtypeStruct((NE, CAP, 128), bf),
-            jax.ShapeDtypeStruct((SLICE, HID), bf),
-            jax.ShapeDtypeStruct((SLICE, HID), bf),
+            jax.ShapeDtypeStruct((NE, CAP, D), bf),
+            jax.ShapeDtypeStruct((NE, CAP, D), bf),
+            jax.ShapeDtypeStruct((TOK, NE * CAP), bf),
+            jax.ShapeDtypeStruct((TOK, 128), f32),
+            jax.ShapeDtypeStruct((SLICE, 2 * HID), bf),
             jax.ShapeDtypeStruct((HID, SLICE), bf),
         ),
-        in_specs=[any_] * 5,
-        out_specs=(any_, any_, vm, vm, vm),
+        in_specs=[vm] * 2 + [any_] * 5,
+        out_specs=(any_, any_, any_, vm, vm, any_, any_),
         scratch_shapes=[
+            pltpu.VMEM((2, TOK, D), bf),
+            pltpu.VMEM((2, NE, CAP, SC), bf),
+            pltpu.VMEM((SLICE, 2 * HID), bf),
+            pltpu.VMEM((HID, SLICE), bf),
+            pltpu.VMEM((NE * CAP, TOK), bf),
+            pltpu.VMEM((NE * CAP, TOK), bf),
+            pltpu.VMEM((NE * CAP, TOK), bf),
+            pltpu.VMEM((NE * CAP, TOK), bf),
+            pltpu.VMEM((NE, CAP, 128), bf),
             pltpu.VMEM((NE, CAP, D), bf),
             pltpu.VMEM((NE, CAP, D), bf),
             pltpu.VMEM((NE, CAP, D), bf),
@@ -294,49 +402,60 @@
             pltpu.VMEM((NZ - 1, NE * CAP, 2 * HID), bf),
             pltpu.VMEM((NE * CAP, 2 * HID), bf),
             pltpu.VMEM((NE * CAP, HID), bf),
-            pltpu.VMEM((NZ - 1, HID, SLICE), bf),
-            pltpu.VMEM((NZ - 1, HID, SLICE), bf),
-            pltpu.VMEM((ROWS, HID), jnp.float32),
-            pltpu.VMEM((ROWS, HID), jnp.float32),
-            dma((3,)), dma((4,)), dma((GROUPS,)), dma((GROUPS,)),
-        ] + [dma] * 12,
+            pltpu.VMEM((2, HID, SLICE), bf),
+            pltpu.VMEM((2, HID // 2, SLICE), bf),
+            pltpu.VMEM((ROWS, HID), f32),
+            pltpu.VMEM((ROWS, HID), f32),
+            dma((2,)), dma((2,)), dma((2,)), dma((3,)), dma((4,)), dma((GROUPS,)), dma((GROUPS,)),
+        ] + [dma] * 6 + [dma] * 2 + [dma((GROUPS,)), dma((GROUPS,)), dma, dma, dma, dma((2,)), dma],
         compiler_params=pltpu.CompilerParams(
-            collective_id=0, has_side_effects=True, vmem_limit_bytes=63 * 2**20
-        ),
-    )(send_x, send_dy, w_gate, w_up, w_down)
+            collective_id=0, has_side_effects=True, vmem_limit_bytes=VMEM_BYTES
+        ),
+    )(ids_t, weight_t, tokens, grad_out, w_gate, w_up, w_down)
+
+
+def finish_kernel(put_t, back, wide, down, grad_tokens, grad_gate, grad_up, grad_down):
+    grad_tokens[...] = jnp.dot(put_t[...], back[...], preferred_element_type=jnp.float32).astype(jnp.bfloat16)
+    grad_gate[...] = wide[:, :HID]
+    grad_up[...] = wide[:, HID:]
+    grad_down[...] = down[...]
+
+
+def finish(put_t, back, wide, down):
+    bf = jnp.bfloat16
+    steps = 8
+    return pl.pallas_call(
+        finish_kernel,
+        grid=(steps,),
+        out_shape=(
+            jax.ShapeDtypeStruct((TOK, D), bf),
+            jax.ShapeDtypeStruct((SLICE, HID), bf),
+            jax.ShapeDtypeStruct((SLICE, HID), bf),
+            jax.ShapeDtypeStruct((HID, SLICE), bf),
+        ),
+        in_specs=[
+            pl.BlockSpec((TOK, NE * CAP), lambda k: (0, 0)),
+            pl.BlockSpec((NE * CAP, D // steps), lambda k: (0, k)),
+            pl.BlockSpec((SLICE // steps, 2 * HID), lambda k: (k, 0)),
+            pl.BlockSpec((HID // steps, SLICE), lambda k: (k, 0)),
+        ],
+        out_specs=(
+            pl.BlockSpec((TOK, D // steps), lambda k: (0, k)),
+            pl.BlockSpec((SLICE // steps, HID), lambda k: (k, 0)),
+            pl.BlockSpec((SLICE // steps, HID), lambda k: (k, 0)),
+            pl.BlockSpec((HID // steps, SLICE), lambda k: (k, 0)),
+        ),
+        compiler_params=pltpu.CompilerParams(vmem_limit_bytes=60 * 2**20),
+    )(put_t, back, wide, down)
 
 
 def on_device(tokens, grad_out, expert_ids, combine, w_gate, w_up, w_down):
-    bf = jnp.bfloat16
-    rows = tokens.shape[0]
-    labels = jnp.arange(NE, dtype=jnp.int32)
-    hits = [(expert_ids[:, k, None] == labels[None, :]).astype(bf) for k in range(2)]
-    order = jnp.arange(rows, dtype=jnp.int32)
-    before = (order[None, :] < order[:, None]).astype(bf)
-    earlier = jnp.dot(before, hits[0] + hits[1], preferred_element_type=jnp.float32)
-    places = [
-        expert_ids[:, k] * CAP + jnp.sum(earlier * hits[k].astype(jnp.float32), axis=1).astype(jnp.int32)
-        for k in range(2)
-    ]
-    slots = jnp.arange(NE * CAP, dtype=jnp.int32)
-    put = [(slots[:, None] == places[k][None, :]).astype(bf) for k in range(2)]
-    put_x = put[0] + put[1]
-    put_dy = put[0] * combine[:, 0][None, :] + put[1] * combine[:, 1][None, :]
-    send_x = jnp.dot(put_x, tokens, preferred_element_type=jnp.float32).astype(bf)
-    send_dy = jnp.dot(put_dy, grad_out, preferred_element_type=jnp.float32).astype(bf)
-    back, back_c, grad_gate, grad_up, grad_down = exchange(
-        send_x.reshape(NE, CAP, D), send_dy.reshape(NE, CAP, D), w_gate[0], w_up[0], w_down[0]
+    back, _, _, put_t, sums, wide, down = exchange(
+        expert_ids.T, combine.T, tokens, grad_out, w_gate[0], w_up[0], w_down[0]
     )
-    grad_tokens = lax.dot_general(
-        put_x, back.reshape(NE * CAP, D), (((0,), (0,)), ((), ())), preferred_element_type=jnp.float32
-    ).astype(bf)
-    sums = back_c.reshape(NE * CAP, 128)
-    parts = [
-        lax.dot_general(put[k], sums, (((0,), (0,)), ((), ())), preferred_element_type=jnp.float32)
-        for k in range(2)
-    ]
-    grad_combine = jnp.stack([p[:, 0] + p[:, 64] for p in parts], axis=1) / combine.astype(jnp.float32)
-    return grad_tokens, grad_combine.astype(bf), grad_gate[None], grad_up[None], grad_down[None]
+    grad_tokens, grad_gate, grad_up, grad_down = finish(put_t, back.reshape(NE * CAP, D), wide, down)
+    grad_combine = (sums[:, :2] / combine.astype(jnp.float32)).astype(jnp.bfloat16)
+    return grad_tokens, grad_combine, grad_gate[None], grad_up[None], grad_down[None]
 
 
 def solution(mesh):

time: 278 us -> 267 us (0.960)
  the two profiles are of different devices: /device:TPU:123 before, /device:TPU:67 now
where the time goes in v2:
time: 267 us; the launch traced here: 265 us
  Pallas kernels  263 us (99%)
    pallas_call x1, Pallas kernels, exchange(): pl.pallas_call(kernel, out_shape=(jax.ShapeDtypeStruct((NE, CAP, D), bf),...  254 us
    pallas_call x1, Pallas kernels, finish(): pl.pallas_call(finish_kernel, grid=(steps,), out_shape=(jax.ShapeDtypeStr...  8.97 us

profile of v2, /device:TPU:67, one launch (start us, length us, event | category | flops | bytes accessed | tf_op | source)
XLA Modules:
  0.0 264.7 jit_solution(14201349343006049150)
XLA Ops:
  0.6 254.1 %shard_map.110 = (bf16[32,24,4096]{2,1,0:T(8,128)(2,1)}, bf16[32,24,4096]{2,1,0:T(8,128)(2,1)}, bf16[32,24,4096]{2,1,0:T(8,128)(2,1)}, bf16[256,768]{1,0:T(8,128...) custom-call(s32[2,256]{1,0:T(2,128)} %bitcast.16, bf16[2,256]{1,0:T(2,128)(2,1)} %bitcast.15, ...), custom_call_target="tpu_custom_call" | custom-call | tf_op jit(solution)/shard_map/pallas_call | solution.py:371
  254.7 0.0 copy-start
  254.8 0.0 copy-start.1
  254.8 9.0 %shard_map.111 = (bf16[256,4096]{1,0:T(8,128)(2,1)}, bf16[1024,512]{1,0:T(8,128)(2,1)}, bf16[1024,512]{1,0:T(8,128)(2,1)}, bf16[512,1024]{1,0:T(8,128)(2,1)}) custom-call(bf16[256,768]{1,0:T(8,128)(2,1)} %get-tuple-element.14.put_t, bf16[768,4096]{1,0:T(8,128)(2,1)} %bitcast.10, bf16[1024,1024]{1,0:T(8,128)(2,1)} %get-tuple-element.16.wide, ...), custom_call_target="tpu_custom_call" | custom-call | tf_op jit(solution)/shard_map/pallas_call | solution.py:427
  263.7 0.0 copy-done
  263.8 0.1 copy.12
  263.8 0.0 copy-done.1
  263.9 0.1 copy.13
  264.0 0.7 copy.14
  (1 shorter events, 0.0 us)
Async XLA Ops:
  254.7 9.0 %copy-start = (f32[256,128]{1,0:T(8,128)S(1)}, f32[256,128]{1,0:T(8,128)}, u32[]{:S(2)}) copy-start(f32[256,128]{1,0:T(8,128)} %get-tuple-element.19) | copy-start | bytes 393220
  254.8 9.1 %copy-start.1 = (bf16[256,2]{0,1:T(2,128)(2,1)S(1)}, bf16[256,2]{0,1:T(2,128)(2,1)}, u32[]{:S(2)}) copy-start(bf16[256,2]{0,1:T(2,128)(2,1)} %param.10) | copy-start | bytes 3076

commit v3 on v2

--- a/solution.py
+++ b/solution.py
@@ -14,7 +14,8 @@
 GROUPS = NE // GROUP
 ROWS = GROUP * CAP
 TOK = 256
-SC = 512
+PARTNER, OWN = NE - 2, NE - 1
+SC = 2048
 VMEM_BYTES = 63 * 2**20
 RETURNS = {2: range(0, 8), 3: range(8, 24)}
 OFFSETS = (
@@ -58,8 +59,8 @@
         pltpu.make_async_copy(wg_h, wg, w_sem.at[0]),
         pltpu.make_async_copy(wu_h, wu, w_sem.at[1]),
         pltpu.make_async_copy(wd_h, wd, w_sem.at[2]),
-        pltpu.make_async_copy(sx.at[ex], xr.at[0], loc_sem.at[0]),
-        pltpu.make_async_copy(sdy.at[ex], dyr.at[0], loc_sem.at[1]),
+        pltpu.make_async_copy(sx.at[OWN], xr.at[OWN], loc_sem.at[0]),
+        pltpu.make_async_copy(sdy.at[OWN], dyr.at[OWN], loc_sem.at[1]),
     ]
 
     barrier = pltpu.get_barrier_semaphore()
@@ -77,13 +78,19 @@
 
     ids = [ids_t[k : k + 1, :].astype(f32) for k in range(2)]
     weight = weight_t[...].astype(f32)
-    label = lax.broadcasted_iota(jnp.int32, (NE, TOK), 0).astype(f32)
+    position = lax.broadcasted_iota(jnp.int32, (NE, TOK), 0)
+    label = jnp.where(position == OWN, ex, ex + 1 - 2 * c)
+    for n in range(PARTNER):
+        dx, dy = offset(n // 2, c)
+        label = jnp.where(position == n, expert_at(x + dx, y + dy, n % 2), label)
+    label = label.astype(f32)
+    position = position.astype(f32)
     hits = [(label == ids[k]).astype(f32) for k in range(2)]
     first = lax.broadcasted_iota(jnp.int32, (TOK, TOK), 0)
     second = lax.broadcasted_iota(jnp.int32, (TOK, TOK), 1)
     before = (first < second).astype(f32).astype(bf)
     earlier = jnp.dot((hits[0] + hits[1]).astype(bf), before, preferred_element_type=f32)
-    places = [ids[k] * CAP + jnp.sum(earlier * hits[k], axis=0, keepdims=True) for k in range(2)]
+    places = [jnp.sum((position * CAP + earlier) * hits[k], axis=0, keepdims=True) for k in range(2)]
     index = lax.broadcasted_iota(jnp.int32, (NE * CAP, TOK), 0).astype(f32)
     put_k = [(index == places[k]).astype(f32) for k in range(2)]
     put[...] = (put_k[0] + put_k[1]).astype(bf)
@@ -91,52 +98,58 @@
     put1[...] = put_k[1].astype(bf)
     put_dy[...] = (put_k[0] * weight[0:1] + put_k[1] * weight[1:2]).astype(bf)
 
-    def lay_out(which, rows, dst):
-        def block(k, carry):
-            kk = pl.ds(pl.multiple_of(k * SC, SC), SC)
-            half = k % 2
-            move = pltpu.make_async_copy(stage.at[half], dst.at[:, :, kk], st_sem.at[half])
-
-            @pl.when(k >= 2)
-            def _():
-                move.wait()
-
-            made = jnp.dot(rows[...], tokdy[which, :, kk], preferred_element_type=f32)
-            stage[half] = made.astype(bf).reshape(NE, CAP, SC)
-            move.start()
-            return carry
-
-        fetch[which].wait()
-        lax.fori_loop(0, D // SC, block, 0)
-        for half in range(2):
-            pltpu.make_async_copy(stage.at[half], dst.at[:, :, pl.ds(0, SC)], st_sem.at[half]).wait()
-        loads[3 + which].start()
-
-    def to_expert(src, dst, send, recv, i, core):
-        if i < 0:
-            to, slot = ex + 1 - 2 * c, 1
-            group = 0
+    def to_expert(src, dst, send, recv, n):
+        if n == PARTNER:
+            to, slot = ex + 1 - 2 * c, PARTNER
         else:
+            i, core = n // 2, n % 2
             dx, dy = offset(i, c)
-            to, slot = expert_at(x + dx, y + dy, core), 2 + 2 * i + c
-            group = (2 + 2 * i) // GROUP
+            to, slot = expert_at(x + dx, y + dy, core), 2 * i + c
         return pltpu.make_async_remote_copy(
-            src_ref=src.at[to], dst_ref=dst.at[slot], send_sem=send, recv_sem=recv.at[group],
+            src_ref=src.at[n], dst_ref=dst.at[slot], send_sem=send, recv_sem=recv.at[n // GROUP],
             device_id=(z, to), device_id_type=MESH,
         )
 
-    lay_out(0, put, sx)
-    pl.semaphore_wait(barrier, NE - 1 + NZ - 1)
-    for g in range(GROUPS):
-        for src, dst, send, recv in ((sx, xr, x_send, x_recv), (sdy, dyr, dy_send, dy_recv)):
-            if g == 0 and src is sdy:
-                lay_out(1, put_dy, sdy)
-            for slot in range(GROUP * g, GROUP * (g + 1), 2):
-                if slot == 0:
-                    to_expert(src, dst, send, recv, -1, 0).start()
-                else:
-                    for core in range(2):
-                        to_expert(src, dst, send, recv, (slot - 2) // 2, core).start()
+    kinds = ((put, sx, xr, x_send, x_recv), (put_dy, sdy, dyr, dy_send, dy_recv))
+
+    def stage_out(step, h):
+        g, which = divmod(step, 2)
+        kk = pl.ds(pl.multiple_of(h * SC, SC), SC)
+        return pltpu.make_async_copy(
+            stage.at[h], kinds[which][1].at[pl.ds(GROUP * g, GROUP), :, kk], st_sem.at[h]
+        )
+
+    def leave(step):
+        g, which = divmod(step, 2)
+        _, src, dst, send, recv = kinds[which]
+        for n in range(GROUP * g, GROUP * (g + 1)):
+            if n == OWN:
+                loads[3 + which].start()
+            else:
+                to_expert(src, dst, send, recv, n).start()
+
+    for step in range(2 * GROUPS):
+        g, which = divmod(step, 2)
+        if g == 0:
+            fetch[which].wait()
+
+        def lay_out(h, carry):
+            if step > 0:
+                stage_out(step - 1, h).wait()
+            kk = pl.ds(pl.multiple_of(h * SC, SC), SC)
+            made = jnp.dot(kinds[which][0][pl.ds(g * ROWS, ROWS), :], tokdy[which, :, kk], preferred_element_type=f32)
+            stage[h] = made.reshape(GROUP, CAP, SC).astype(bf)
+            stage_out(step, h).start()
+            return carry
+
+        lax.fori_loop(0, D // SC, lay_out, 0)
+        if step == 1:
+            pl.semaphore_wait(barrier, NE - 1 + NZ - 1)
+        if step > 0:
+            leave(step - 1)
+    for h in range(D // SC):
+        stage_out(2 * GROUPS - 1, h).wait()
+    leave(2 * GROUPS - 1)
 
     def wait_recv(dst, sem):
         pltpu.make_async_remote_copy(
@@ -151,12 +164,12 @@
         ).wait_send()
 
     def arrive(dst, recv, own, g):
-        @pl.when(g == 0)
+        @pl.when(g == GROUPS - 1)
         def _():
             loads[own].wait()
-            wait_recv(dst.at[pl.ds(1, GROUP - 1)], recv.at[0])
-
-        @pl.when(g > 0)
+            wait_recv(dst.at[pl.ds(NE - GROUP, GROUP - 1)], recv.at[GROUPS - 1])
+
+        @pl.when(g < GROUPS - 1)
         def _():
             wait_recv(dst.at[pl.ds(GROUP * g, GROUP)], recv.at[g])
 
@@ -167,20 +180,20 @@
         )
 
     def give_back(slot):
-        if slot == 0:
+        if slot == OWN:
             return [
-                pltpu.make_async_copy(pg.at[0], back.at[ex], loc_sem.at[2]),
-                pltpu.make_async_copy(pc.at[0], back_c.at[ex], loc_sem.at[3]),
+                pltpu.make_async_copy(pg.at[OWN], back.at[OWN], loc_sem.at[2]),
+                pltpu.make_async_copy(pc.at[OWN], back_c.at[OWN], loc_sem.at[3]),
             ]
-        if slot == 1:
-            to = ex + 1 - 2 * c
+        if slot == PARTNER:
+            to, n = ex + 1 - 2 * c, PARTNER
         else:
-            i, core = (slot - 2) // 2, slot % 2
+            i, core = slot // 2, slot % 2
             dx, dy = offset(i, core)
-            to = expert_at(x - dx, y - dy, core)
+            to, n = expert_at(x - dx, y - dy, core), 2 * i + c
         return [
             pltpu.make_async_remote_copy(
-                src_ref=src.at[slot], dst_ref=dst.at[ex], send_sem=send, recv_sem=recv,
+                src_ref=src.at[slot], dst_ref=dst.at[n], send_sem=send, recv_sem=recv,
                 device_id=(z, to), device_id_type=MESH,
             )
             for src, dst, send, recv in ((pg, back, pg_send, pg_recv), (pc, back_c, pc_send, pc_recv))
@@ -236,8 +249,6 @@
         def _():
             pass_on(g - 1)
 
-        arrive(dyr, dy_recv, 4, g)
-
         for step, slots in RETURNS.items():
 
             @pl.when(g == step)
@@ -245,6 +256,8 @@
                 for slot in slots:
                     for copy in give_back(slot):
                         copy.start()
+
+        arrive(dyr, dy_recv, 4, g)
 
         def backward(k, hg):
             kk = pl.ds(pl.multiple_of(k * KC, KC), KC)
@@ -261,13 +274,13 @@
         high = total.astype(jnp.bfloat16).astype(jnp.float32)
         lane = lax.broadcasted_iota(jnp.int32, (ROWS, 128), 1)
         pc[pl.ds(base, GROUP)] = (
-            jnp.where(lane < 64, high, total - high).astype(jnp.bfloat16).reshape(GROUP, CAP, 128)
+            jnp.where(lane < 64, high, total - high).reshape(GROUP, CAP, 128).astype(jnp.bfloat16)
         )
 
         def inward(k, cc):
             kk = pl.ds(pl.multiple_of(k * KC, KC), KC)
             part = nt(gown[rows, pl.ds(0, HID)], wg[kk, :]) + nt(gown[rows, pl.ds(HID, HID)], wu[kk, :])
-            pg[pl.ds(base, GROUP), :, kk] = part.astype(jnp.bfloat16).reshape(GROUP, CAP, KC)
+            pg[pl.ds(base, GROUP), :, kk] = part.reshape(GROUP, CAP, KC).astype(jnp.bfloat16)
             return cc
 
         lax.fori_loop(0, D // KC, inward, 0)
@@ -347,17 +360,13 @@
     wait_send(tokdy.at[:, :, pl.ds(0, (NZ - 1) * SLICE)], dn_send)
     wait_send(pg.at[most], pg_send)
     wait_send(pc.at[most], pc_send)
-    for copy in give_back(0):
+    for copy in give_back(OWN):
         copy.wait()
     wait_recv(back_c.at[most], pc_recv)
     sums = back_c[...].reshape(NE * CAP, 128)
-    both = [tn(rows[...], sums) for rows in (put0, put1)]
-    lane = lax.broadcasted_iota(jnp.int32, (TOK, 128), 1)
-    out_c[...] = jnp.where(
-        lane == 0,
-        jnp.sum(jnp.where(lane % 64 == 0, both[0], 0.0), axis=1, keepdims=True),
-        jnp.sum(jnp.where(lane % 64 == 0, both[1], 0.0), axis=1, keepdims=True),
-    )
+    for k, rows in ((0, put0), (1, put1)):
+        both = tn(sums, rows[...])
+        out_c[k : k + 1, :] = (both[0:1] + both[64:65]) / weight_t[k : k + 1, :].astype(f32)
     wait_recv(back.at[most], pg_recv)
     wide_out.wait()
     down_out.wait()
@@ -375,7 +384,7 @@
             jax.ShapeDtypeStruct((NE, CAP, D), bf),
             jax.ShapeDtypeStruct((NE, CAP, D), bf),
             jax.ShapeDtypeStruct((TOK, NE * CAP), bf),
-            jax.ShapeDtypeStruct((TOK, 128), f32),
+            jax.ShapeDtypeStruct((2, TOK), f32),
             jax.ShapeDtypeStruct((SLICE, 2 * HID), bf),
             jax.ShapeDtypeStruct((HID, SLICE), bf),
         ),
@@ -383,7 +392,7 @@
         out_specs=(any_, any_, any_, vm, vm, any_, any_),
         scratch_shapes=[
             pltpu.VMEM((2, TOK, D), bf),
-            pltpu.VMEM((2, NE, CAP, SC), bf),
+            pltpu.VMEM((D // SC, GROUP, CAP, SC), bf),
             pltpu.VMEM((SLICE, 2 * HID), bf),
             pltpu.VMEM((HID, SLICE), bf),
             pltpu.VMEM((NE * CAP, TOK), bf),
@@ -414,48 +423,73 @@
     )(ids_t, weight_t, tokens, grad_out, w_gate, w_up, w_down)
 
 
-def finish_kernel(put_t, back, wide, down, grad_tokens, grad_gate, grad_up, grad_down):
-    grad_tokens[...] = jnp.dot(put_t[...], back[...], preferred_element_type=jnp.float32).astype(jnp.bfloat16)
-    grad_gate[...] = wide[:, :HID]
-    grad_up[...] = wide[:, HID:]
-    grad_down[...] = down[...]
-
-
-def finish(put_t, back, wide, down):
+def finish_kernel(
+    put_t, sums, back, wide, down, grad_tokens, grad_combine, grad_gate, grad_up, grad_down,
+    rows, made, wide_v, down_v, load_sem, out_sem,
+):
+    steps = 4
+    width = D // steps
+    loads = [
+        pltpu.make_async_copy(back.at[:, :, pl.ds(k * width, width)], rows.at[:, :, pl.ds(k * width, width)], load_sem.at[k])
+        for k in range(steps)
+    ]
+    loads.append(pltpu.make_async_copy(wide, wide_v, load_sem.at[steps]))
+    loads.append(pltpu.make_async_copy(down, down_v, load_sem.at[steps + 1]))
+    for copy in loads:
+        copy.start()
+    moves = []
+    grad_combine[...] = sums[...].astype(jnp.bfloat16)
+    for k in range(steps):
+        kk = pl.ds(k * width, width)
+        loads[k].wait()
+        block = rows[:, :, kk].reshape(NE * CAP, width)
+        made[:, kk] = jnp.dot(put_t[...], block, preferred_element_type=jnp.float32).astype(jnp.bfloat16)
+        moves.append(pltpu.make_async_copy(made.at[:, kk], grad_tokens.at[:, kk], out_sem.at[3 + k]))
+        moves[-1].start()
+    loads[steps].wait()
+    loads[steps + 1].wait()
+    for src, dst, sem in (
+        (wide_v.at[:, pl.ds(0, HID)], grad_gate, 0), (wide_v.at[:, pl.ds(HID, HID)], grad_up, 1), (down_v, grad_down, 2),
+    ):
+        moves.append(pltpu.make_async_copy(src, dst, out_sem.at[sem]))
+        moves[-1].start()
+    for copy in moves:
+        copy.wait()
+
+
+def finish(put_t, sums, back, wide, down):
     bf = jnp.bfloat16
-    steps = 8
+    any_ = pl.BlockSpec(memory_space=pl.ANY)
+    vm = pl.BlockSpec(memory_space=pltpu.VMEM)
     return pl.pallas_call(
         finish_kernel,
-        grid=(steps,),
         out_shape=(
             jax.ShapeDtypeStruct((TOK, D), bf),
+            jax.ShapeDtypeStruct((2, TOK), bf),
             jax.ShapeDtypeStruct((SLICE, HID), bf),
             jax.ShapeDtypeStruct((SLICE, HID), bf),
             jax.ShapeDtypeStruct((HID, SLICE), bf),
         ),
-        in_specs=[
-            pl.BlockSpec((TOK, NE * CAP), lambda k: (0, 0)),
-            pl.BlockSpec((NE * CAP, D // steps), lambda k: (0, k)),
-            pl.BlockSpec((SLICE // steps, 2 * HID), lambda k: (k, 0)),
-            pl.BlockSpec((HID // steps, SLICE), lambda k: (k, 0)),
+        in_specs=[vm, vm, any_, any_, any_],
+        out_specs=(any_, vm, any_, any_, any_),
+        scratch_shapes=[
+            pltpu.VMEM((NE, CAP, D), bf),
+            pltpu.VMEM((TOK, D), bf),
+            pltpu.VMEM((SLICE, 2 * HID), bf),
+            pltpu.VMEM((HID, SLICE), bf),
+            pltpu.SemaphoreType.DMA((6,)),
+            pltpu.SemaphoreType.DMA((7,)),
         ],
-        out_specs=(
-            pl.BlockSpec((TOK, D // steps), lambda k: (0, k)),
-            pl.BlockSpec((SLICE // steps, HID), lambda k: (k, 0)),
-            pl.BlockSpec((SLICE // steps, HID), lambda k: (k, 0)),
-            pl.BlockSpec((HID // steps, SLICE), lambda k: (k, 0)),
-        ),
         compiler_params=pltpu.CompilerParams(vmem_limit_bytes=60 * 2**20),
-    )(put_t, back, wide, down)
+    )(put_t, sums, back, wide, down)
 
 
 def on_device(tokens, grad_out, expert_ids, combine, w_gate, w_up, w_down):
     back, _, _, put_t, sums, wide, down = exchange(
         expert_ids.T, combine.T, tokens, grad_out, w_gate[0], w_up[0], w_down[0]
     )
-    grad_tokens, grad_gate, grad_up, grad_down = finish(put_t, back.reshape(NE * CAP, D), wide, down)
-    grad_combine = (sums[:, :2] / combine.astype(jnp.float32)).astype(jnp.bfloat16)
-    return grad_tokens, grad_combine, grad_gate[None], grad_up[None], grad_down[None]
+    grad_tokens, grad_combine, grad_gate, grad_up, grad_down = finish(put_t, sums, back, wide, down)
+    return grad_tokens, grad_combine.T, grad_gate[None], grad_up[None], grad_down[None]
 
 
 def solution(mesh):

time: 267 us -> 258 us (0.966)
  Pallas kernels: 263 us -> 257 us
    pallas_call x1, Pallas kernels: 254 us -> 250 us  [exchange(): pl.pallas_call(kernel, out_shape=(jax.ShapeDtypeStruct((NE, CAP, D), bf),...]
where the time goes in v3:
time: 258 us
  Pallas kernels  257 us (100%)
    pallas_call x1, Pallas kernels, exchange(): pl.pallas_call(kernel, out_shape=(jax.ShapeDtypeStruct((NE, CAP, D), bf),...  250 us
    pallas_call x1, Pallas kernels, finish(): pl.pallas_call(finish_kernel, out_shape=(jax.ShapeDtypeStruct((TOK, D), b...  7.45 us

profile of v3, /device:TPU:67, one launch (start us, length us, event | category | flops | bytes accessed | tf_op | source)
XLA Modules:
  0.0 258.1 jit_solution(12577869335152360757)
XLA Ops:
  0.6 250.0 %shard_map.110 = (bf16[32,24,4096]{2,1,0:T(8,128)(2,1)}, bf16[32,24,4096]{2,1,0:T(8,128)(2,1)}, bf16[32,24,4096]{2,1,0:T(8,128)(2,1)}, bf16[256,768]{1,0:T(8,128...) custom-call(s32[2,256]{1,0:T(2,128)} %bitcast.12, bf16[2,256]{1,0:T(2,128)(2,1)} %bitcast.13, ...), custom_call_target="tpu_custom_call" | custom-call | tf_op jit(solution)/shard_map/pallas_call | solution.py:380
  250.6 7.5 %shard_map.111 = (bf16[256,4096]{1,0:T(8,128)(2,1)}, bf16[2,256]{1,0:T(2,128)(2,1)}, bf16[1024,512]{1,0:T(8,128)(2,1)}, bf16[1024,512]{1,0:T(8,128)(2,1)}, bf16[512,1024]{1,0:T(8,128)(2,1)}) custom-call(bf16[256,768]{1,0:T(8,128)(2,1)} %get-tuple-element.15.put_t, f32[2,256]{1,0:T(2,128)} %get-tuple-element.16.sums, ...), custom_call_target="tpu_custom_call" | custom-call | tf_op jit(solution)/shard_map/pallas_call | solution.py:464

commit v4 on v3

--- a/solution.py
+++ b/solution.py
@@ -17,7 +17,6 @@
 PARTNER, OWN = NE - 2, NE - 1
 SC = 2048
 VMEM_BYTES = 63 * 2**20
-RETURNS = {2: range(0, 8), 3: range(8, 24)}
 OFFSETS = (
     (1, 0), (3, 0), (0, 1), (0, 3), (1, 1), (3, 3), (1, 3), (3, 1),
     (2, 0), (0, 2), (1, 2), (3, 2), (2, 1), (2, 3), (2, 2),
@@ -113,14 +112,14 @@
     kinds = ((put, sx, xr, x_send, x_recv), (put_dy, sdy, dyr, dy_send, dy_recv))
 
     def stage_out(step, h):
-        g, which = divmod(step, 2)
+        which, g = divmod(step, GROUPS)
         kk = pl.ds(pl.multiple_of(h * SC, SC), SC)
         return pltpu.make_async_copy(
             stage.at[h], kinds[which][1].at[pl.ds(GROUP * g, GROUP), :, kk], st_sem.at[h]
         )
 
     def leave(step):
-        g, which = divmod(step, 2)
+        which, g = divmod(step, GROUPS)
         _, src, dst, send, recv = kinds[which]
         for n in range(GROUP * g, GROUP * (g + 1)):
             if n == OWN:
@@ -129,7 +128,7 @@
                 to_expert(src, dst, send, recv, n).start()
 
     for step in range(2 * GROUPS):
-        g, which = divmod(step, 2)
+        which, g = divmod(step, GROUPS)
         if g == 0:
             fetch[which].wait()
 
@@ -215,16 +214,21 @@
         high = pl.ds(pl.multiple_of(g * ROWS + ROWS // 2, ROWS // 2), ROWS // 2)
         over_z(gz.at[2, high], gz.at[1, high], gz_send, gz_far, 3).start()
 
-    KC = 1024
-
-    def group_step(g, carry):
+    def spread(g, carry):
         base = pl.multiple_of(GROUP * g, GROUP)
-        rows = pl.ds(pl.multiple_of(g * ROWS, ROWS), ROWS)
         arrive(xr, x_recv, 3, g)
         for j in (2, 1, 3):
             cols = pl.ds(pl.multiple_of((z + j) % NZ * SLICE, SLICE), SLICE)
             over_z(xr.at[pl.ds(base, GROUP), :, cols], xz.at[j - 1, pl.ds(base, GROUP)], xz_send, xz_recv, j).start()
-
+        return carry
+
+    lax.fori_loop(0, GROUPS, spread, 0)
+
+    KC = 1024
+
+    def group_step(g, carry):
+        base = pl.multiple_of(GROUP * g, GROUP)
+        rows = pl.ds(pl.multiple_of(g * ROWS, ROWS), ROWS)
         fa[...] = jnp.zeros_like(fa)
         fb[...] = jnp.zeros_like(fb)
 
@@ -248,14 +252,6 @@
         @pl.when(g >= 1)
         def _():
             pass_on(g - 1)
-
-        for step, slots in RETURNS.items():
-
-            @pl.when(g == step)
-            def _():
-                for slot in slots:
-                    for copy in give_back(slot):
-                        copy.start()
 
         arrive(dyr, dy_recv, 4, g)
 
@@ -284,12 +280,17 @@
             return cc
 
         lax.fori_loop(0, D // KC, inward, 0)
+        for done in range(GROUPS):
+
+            @pl.when(g == done)
+            def _():
+                for slot in range(GROUP * done, GROUP * (done + 1)):
+                    for copy in give_back(slot):
+                        copy.start()
+
         return carry
 
     lax.fori_loop(0, GROUPS, group_step, 0)
-    for slot in range(NE - GROUP, NE):
-        for copy in give_back(slot):
-            copy.start()
 
     pass_on(GROUPS - 1)
 

time: 258 us -> 243 us (0.942)
  Pallas kernels: 257 us -> 240 us
    pallas_call x1, Pallas kernels: 250 us -> 233 us  [exchange(): pl.pallas_call(kernel, out_shape=(jax.ShapeDtypeStruct((NE, CAP, D), bf),...]
where the time goes in v4:
time: 243 us; the launch traced here: 241 us
  Pallas kernels  240 us (99%)
    pallas_call x1, Pallas kernels, exchange(): pl.pallas_call(kernel, out_shape=(jax.ShapeDtypeStruct((NE, CAP, D), bf),...  233 us
    pallas_call x1, Pallas kernels, finish(): pl.pallas_call(finish_kernel, out_shape=(jax.ShapeDtypeStruct((TOK, D), b...  7.45 us

profile of v4, /device:TPU:67, one launch (start us, length us, event | category | flops | bytes accessed | tf_op | source)
XLA Modules:
  0.0 241.1 jit_solution(12637117100432391172)
XLA Ops:
  0.6 233.0 %shard_map.110 = (bf16[32,24,4096]{2,1,0:T(8,128)(2,1)}, bf16[32,24,4096]{2,1,0:T(8,128)(2,1)}, bf16[32,24,4096]{2,1,0:T(8,128)(2,1)}, bf16[256,768]{1,0:T(8,128...) custom-call(s32[2,256]{1,0:T(2,128)} %bitcast.12, bf16[2,256]{1,0:T(2,128)(2,1)} %bitcast.13, ...), custom_call_target="tpu_custom_call" | custom-call | tf_op jit(solution)/shard_map/pallas_call | solution.py:381
  233.6 7.5 %shard_map.111 = (bf16[256,4096]{1,0:T(8,128)(2,1)}, bf16[2,256]{1,0:T(2,128)(2,1)}, bf16[1024,512]{1,0:T(8,128)(2,1)}, bf16[1024,512]{1,0:T(8,128)(2,1)}, bf16[512,1024]{1,0:T(8,128)(2,1)}) custom-call(bf16[256,768]{1,0:T(8,128)(2,1)} %get-tuple-element.15.put_t, f32[2,256]{1,0:T(2,128)} %get-tuple-element.16.sums, ...), custom_call_target="tpu_custom_call" | custom-call | tf_op jit(solution)/shard_map/pallas_call | solution.py:465

commit v5 on v4

--- a/solution.py
+++ b/solution.py
@@ -13,6 +13,7 @@
 GROUP = 8
 GROUPS = NE // GROUP
 ROWS = GROUP * CAP
+EARLY = NE - GROUP
 TOK = 256
 PARTNER, OWN = NE - 2, NE - 1
 SC = 2048
@@ -42,9 +43,9 @@
 
 def kernel(
     ids_t, weight_t, tok_h, dy_h, wg_h, wu_h, wd_h,
-    back, sx, sdy, put_t, out_c, wide_h, down_h,
+    back, sx, sdy, early_h, put_last, out_c, wide_h, down_h,
     tokdy, stage, out_gu, out_d, put, put0, put1, put_dy, back_c, xr, dyr, pg, pc, wg, wu, wd, xz, gz, gown, hid, dn_in, dn_rel, fa, fb,
-    in_sem, out_sem, st_sem, w_sem, loc_sem, x_recv, dy_recv, x_send, dy_send, pg_recv, pg_send, pc_recv, pc_send,
+    in_sem, out_sem, early_sem, st_sem, w_sem, loc_sem, x_recv, dy_recv, x_send, dy_send, pg_recv, pg_send, pc_recv, pc_send,
     xz_recv, xz_send, gz_next, gz_prev, gz_far, gz_send, dn_recv, rel_recv, dn_send,
 ):
     bf, f32 = jnp.bfloat16, jnp.float32
@@ -195,12 +196,10 @@
                 src_ref=src.at[slot], dst_ref=dst.at[n], send_sem=send, recv_sem=recv,
                 device_id=(z, to), device_id_type=MESH,
             )
-            for src, dst, send, recv in ((pg, back, pg_send, pg_recv), (pc, back_c, pc_send, pc_recv))
+            for src, dst, send, recv in ((pg, back, pg_send, pg_recv.at[slot // GROUP]), (pc, back_c, pc_send, pc_recv))
         ]
 
-    for k in range(NE * CAP // TOK):
-        part = pl.ds(k * TOK, TOK)
-        put_t[:, part] = put[part, :].astype(f32).T.astype(bf)
+    put_last[...] = put[pl.ds(EARLY * CAP, ROWS), :]
 
     for load in loads[:3]:
         load.wait()
@@ -346,6 +345,25 @@
         dn_out(h, j)[...] = (dn_out(h, j)[...].astype(f32) + dn_rel[h].astype(f32)).astype(bf)
         over_z(dn_out(h, j), dn_in.at[h, high if h else low], dn_send, dn_recv, j).start()
     own = down_part(0)
+
+    wait_send(xz, xz_send)
+    wait_send(gz, gz_send)
+    for g in range(GROUPS - 1):
+        part = pl.ds(GROUP * g, GROUP)
+        wait_recv(back.at[part], pg_recv.at[g])
+        pltpu.make_async_copy(back.at[part], xr.at[part], st_sem.at[0]).start()
+        pltpu.make_async_copy(back.at[part], xr.at[part], st_sem.at[0]).wait()
+    early_out = []
+    for j in range(D // SLICE):
+        cols = pl.ds(j * SLICE, SLICE)
+        kept = gz.at[j // 3, pl.ds(j % 3 * TOK, TOK)]
+        for k in range(2):
+            width = SLICE // 2
+            rows = xr[pl.ds(0, EARLY), :, pl.ds(j * SLICE + k * width, width)].reshape(EARLY * CAP, width)
+            kept[:, pl.ds(k * width, width)] = tn(put[pl.ds(0, EARLY * CAP), :], rows).astype(bf)
+        early_out.append(pltpu.make_async_copy(kept, early_h.at[:, cols], early_sem.at[j]))
+        early_out[-1].start()
+
     wait_recv(dn_in, dn_recv)
     for j in range(2):
         own += dn_in[j].astype(f32)
@@ -356,8 +374,6 @@
     most = pl.ds(0, NE - 1)
     wait_send(sx.at[most], x_send)
     wait_send(sdy.at[most], dy_send)
-    wait_send(xz, xz_send)
-    wait_send(gz, gz_send)
     wait_send(tokdy.at[:, :, pl.ds(0, (NZ - 1) * SLICE)], dn_send)
     wait_send(pg.at[most], pg_send)
     wait_send(pc.at[most], pc_send)
@@ -368,7 +384,9 @@
     for k, rows in ((0, put0), (1, put1)):
         both = tn(sums, rows[...])
         out_c[k : k + 1, :] = (both[0:1] + both[64:65]) / weight_t[k : k + 1, :].astype(f32)
-    wait_recv(back.at[most], pg_recv)
+    wait_recv(back.at[pl.ds(EARLY, GROUP - 1)], pg_recv.at[GROUPS - 1])
+    for copy in early_out:
+        copy.wait()
     wide_out.wait()
     down_out.wait()
 
@@ -384,13 +402,14 @@
             jax.ShapeDtypeStruct((NE, CAP, D), bf),
             jax.ShapeDtypeStruct((NE, CAP, D), bf),
             jax.ShapeDtypeStruct((NE, CAP, D), bf),
-            jax.ShapeDtypeStruct((TOK, NE * CAP), bf),
+            jax.ShapeDtypeStruct((TOK, D), bf),
+            jax.ShapeDtypeStruct((ROWS, TOK), bf),
             jax.ShapeDtypeStruct((2, TOK), f32),
             jax.ShapeDtypeStruct((SLICE, 2 * HID), bf),
             jax.ShapeDtypeStruct((HID, SLICE), bf),
         ),
         in_specs=[vm] * 2 + [any_] * 5,
-        out_specs=(any_, any_, any_, vm, vm, any_, any_),
+        out_specs=(any_, any_, any_, any_, vm, vm, any_, any_),
         scratch_shapes=[
             pltpu.VMEM((2, TOK, D), bf),
             pltpu.VMEM((D // SC, GROUP, CAP, SC), bf),
@@ -416,8 +435,8 @@
             pltpu.VMEM((2, HID // 2, SLICE), bf),
             pltpu.VMEM((ROWS, HID), f32),
             pltpu.VMEM((ROWS, HID), f32),
-            dma((2,)), dma((2,)), dma((2,)), dma((3,)), dma((4,)), dma((GROUPS,)), dma((GROUPS,)),
-        ] + [dma] * 6 + [dma] * 2 + [dma((GROUPS,)), dma((GROUPS,)), dma, dma, dma, dma((2,)), dma],
+            dma((2,)), dma((2,)), dma((D // SLICE,)), dma((2,)), dma((3,)), dma((4,)), dma((GROUPS,)), dma((GROUPS,)),
+        ] + [dma, dma, dma((GROUPS,)), dma, dma, dma] + [dma] * 2 + [dma((GROUPS,)), dma((GROUPS,)), dma, dma, dma, dma((2,)), dma],
         compiler_params=pltpu.CompilerParams(
             collective_id=0, has_side_effects=True, vmem_limit_bytes=VMEM_BYTES
         ),
@@ -425,26 +444,29 @@
 
 
 def finish_kernel(
-    put_t, sums, back, wide, down, grad_tokens, grad_combine, grad_gate, grad_up, grad_down,
+    put_last, sums, early, back, wide, down, grad_tokens, grad_combine, grad_gate, grad_up, grad_down,
     rows, made, wide_v, down_v, load_sem, out_sem,
 ):
     steps = 4
     width = D // steps
-    loads = [
-        pltpu.make_async_copy(back.at[:, :, pl.ds(k * width, width)], rows.at[:, :, pl.ds(k * width, width)], load_sem.at[k])
-        for k in range(steps)
-    ]
-    loads.append(pltpu.make_async_copy(wide, wide_v, load_sem.at[steps]))
-    loads.append(pltpu.make_async_copy(down, down_v, load_sem.at[steps + 1]))
-    for copy in loads:
+    cols = [pl.ds(k * width, width) for k in range(steps)]
+    last = pl.ds(EARLY, GROUP)
+    loads = [pltpu.make_async_copy(back.at[last, :, kk], rows.at[:, :, kk], load_sem.at[k]) for k, kk in enumerate(cols)]
+    firsts = [pltpu.make_async_copy(early.at[:, kk], made.at[:, kk], load_sem.at[steps + k]) for k, kk in enumerate(cols)]
+    loads.append(pltpu.make_async_copy(wide, wide_v, load_sem.at[2 * steps]))
+    loads.append(pltpu.make_async_copy(down, down_v, load_sem.at[2 * steps + 1]))
+    for pair in zip(loads, firsts):
+        for copy in pair:
+            copy.start()
+    for copy in loads[steps:]:
         copy.start()
     moves = []
     grad_combine[...] = sums[...].astype(jnp.bfloat16)
-    for k in range(steps):
-        kk = pl.ds(k * width, width)
+    for k, kk in enumerate(cols):
         loads[k].wait()
-        block = rows[:, :, kk].reshape(NE * CAP, width)
-        made[:, kk] = jnp.dot(put_t[...], block, preferred_element_type=jnp.float32).astype(jnp.bfloat16)
+        firsts[k].wait()
+        block = rows[:, :, kk].reshape(ROWS, width)
+        made[:, kk] = (made[:, kk].astype(jnp.float32) + tn(put_last[...], block)).astype(jnp.bfloat16)
         moves.append(pltpu.make_async_copy(made.at[:, kk], grad_tokens.at[:, kk], out_sem.at[3 + k]))
         moves[-1].start()
     loads[steps].wait()
@@ -458,7 +480,7 @@
         copy.wait()
 
 
-def finish(put_t, sums, back, wide, down):
+def finish(put_last, sums, early, back, wide, down):
     bf = jnp.bfloat16
     any_ = pl.BlockSpec(memory_space=pl.ANY)
     vm = pl.BlockSpec(memory_space=pltpu.VMEM)
@@ -471,25 +493,25 @@
             jax.ShapeDtypeStruct((SLICE, HID), bf),
             jax.ShapeDtypeStruct((HID, SLICE), bf),
         ),
-        in_specs=[vm, vm, any_, any_, any_],
+        in_specs=[vm, vm, any_, any_, any_, any_],
         out_specs=(any_, vm, any_, any_, any_),
         scratch_shapes=[
-            pltpu.VMEM((NE, CAP, D), bf),
+            pltpu.VMEM((GROUP, CAP, D), bf),
             pltpu.VMEM((TOK, D), bf),
             pltpu.VMEM((SLICE, 2 * HID), bf),
             pltpu.VMEM((HID, SLICE), bf),
-            pltpu.SemaphoreType.DMA((6,)),
+            pltpu.SemaphoreType.DMA((10,)),
             pltpu.SemaphoreType.DMA((7,)),
         ],
         compiler_params=pltpu.CompilerParams(vmem_limit_bytes=60 * 2**20),
-    )(put_t, sums, back, wide, down)
+    )(put_last, sums, early, back, wide, down)
 
 
 def on_device(tokens, grad_out, expert_ids, combine, w_gate, w_up, w_down):
-    back, _, _, put_t, sums, wide, down = exchange(
+    back, _, _, early, put_last, sums, wide, down = exchange(
         expert_ids.T, combine.T, tokens, grad_out, w_gate[0], w_up[0], w_down[0]
     )
-    grad_tokens, grad_combine, grad_gate, grad_up, grad_down = finish(put_t, sums, back, wide, down)
+    grad_tokens, grad_combine, grad_gate, grad_up, grad_down = finish(put_last, sums, early, back, wide, down)
     return grad_tokens, grad_combine.T, grad_gate[None], grad_up[None], grad_down[None]
 
 

time: 243 us -> 243 us (level)
  no operation moved by 1% of the time
where the time goes in v5:
time: 243 us; the launch traced here: 241 us
  Pallas kernels  240 us (99%)
    pallas_call x1, Pallas kernels, exchange(): pl.pallas_call(kernel, out_shape=(jax.ShapeDtypeStruct((NE, CAP, D), bf),...  233 us
    pallas_call x1, Pallas kernels, finish(): pl.pallas_call(finish_kernel, out_shape=(jax.ShapeDtypeStruct((TOK, D), b...  6.99 us

profile of v5, /device:TPU:67, one launch (start us, length us, event | category | flops | bytes accessed | tf_op | source)
XLA Modules:
  0.0 240.6 jit_solution(4640131248759681431)
XLA Ops:
  0.6 232.8 %shard_map.110 = (bf16[32,24,4096]{2,1,0:T(8,128)(2,1)}, bf16[32,24,4096]{2,1,0:T(8,128)(2,1)}, bf16[32,24,4096]{2,1,0:T(8,128)(2,1)}, bf16[256,4096]{1,0:T(8,12...) custom-call(s32[2,256]{1,0:T(2,128)} %bitcast.12, ...), custom_call_target="tpu_custom_call" | custom-call | tf_op jit(solution)/shard_map/pallas_call | solution.py:399
  233.4 7.0 %shard_map.111 = (bf16[256,4096]{1,0:T(8,128)(2,1)}, bf16[2,256]{1,0:T(2,128)(2,1)}, bf16[1024,512]{1,0:T(8,128)(2,1)}, bf16[1024,512]{1,0:T(8,128)(2,1)}, bf16[512,1024]{1,0:T(8,128)(2,1)}) custom-call(bf16[192,256]{1,0:T(8,128)(2,1)} %get-tuple-element.16.put_last, f32[2,256]{1,0:T(2,128)} %get-tuple-element.17.sums, ...), custom_call_target="tpu_custom_call" | custom-call | tf_op jit(solution)/shard_map/pallas_call | solution.py:487

commit v6 on v5

--- a/solution.py
+++ b/solution.py
@@ -381,9 +381,10 @@
         copy.wait()
     wait_recv(back_c.at[most], pc_recv)
     sums = back_c[...].reshape(NE * CAP, 128)
+    weight = weight_t[...].astype(f32)
     for k, rows in ((0, put0), (1, put1)):
         both = tn(sums, rows[...])
-        out_c[k : k + 1, :] = (both[0:1] + both[64:65]) / weight_t[k : k + 1, :].astype(f32)
+        out_c[k : k + 1, :] = (both[0:1] + both[64:65]) / weight[k : k + 1]
     wait_recv(back.at[pl.ds(EARLY, GROUP - 1)], pg_recv.at[GROUPS - 1])
     for copy in early_out:
         copy.wait()
@@ -445,7 +446,7 @@
 
 def finish_kernel(
     put_last, sums, early, back, wide, down, grad_tokens, grad_combine, grad_gate, grad_up, grad_down,
-    rows, made, wide_v, down_v, load_sem, out_sem,
+    rows, made, wide_v, down_v, put_v, load_sem, out_sem,
 ):
     steps = 4
     width = D // steps
@@ -455,6 +456,8 @@
     firsts = [pltpu.make_async_copy(early.at[:, kk], made.at[:, kk], load_sem.at[steps + k]) for k, kk in enumerate(cols)]
     loads.append(pltpu.make_async_copy(wide, wide_v, load_sem.at[2 * steps]))
     loads.append(pltpu.make_async_copy(down, down_v, load_sem.at[2 * steps + 1]))
+    put_in = pltpu.make_async_copy(put_last, put_v, load_sem.at[2 * steps + 2])
+    put_in.start()
     for pair in zip(loads, firsts):
         for copy in pair:
             copy.start()
@@ -462,11 +465,12 @@
         copy.start()
     moves = []
     grad_combine[...] = sums[...].astype(jnp.bfloat16)
+    put_in.wait()
     for k, kk in enumerate(cols):
         loads[k].wait()
         firsts[k].wait()
         block = rows[:, :, kk].reshape(ROWS, width)
-        made[:, kk] = (made[:, kk].astype(jnp.float32) + tn(put_last[...], block)).astype(jnp.bfloat16)
+        made[:, kk] = (made[:, kk].astype(jnp.float32) + tn(put_v[...], block)).astype(jnp.bfloat16)
         moves.append(pltpu.make_async_copy(made.at[:, kk], grad_tokens.at[:, kk], out_sem.at[3 + k]))
         moves[-1].start()
     loads[steps].wait()
@@ -493,14 +497,15 @@
             jax.ShapeDtypeStruct((SLICE, HID), bf),
             jax.ShapeDtypeStruct((HID, SLICE), bf),
         ),
-        in_specs=[vm, vm, any_, any_, any_, any_],
+        in_specs=[any_, vm, any_, any_, any_, any_],
         out_specs=(any_, vm, any_, any_, any_),
         scratch_shapes=[
             pltpu.VMEM((GROUP, CAP, D), bf),
             pltpu.VMEM((TOK, D), bf),
             pltpu.VMEM((SLICE, 2 * HID), bf),
             pltpu.VMEM((HID, SLICE), bf),
-            pltpu.SemaphoreType.DMA((10,)),
+            pltpu.VMEM((ROWS, TOK), bf),
+            pltpu.SemaphoreType.DMA((11,)),
             pltpu.SemaphoreType.DMA((7,)),
         ],
         compiler_params=pltpu.CompilerParams(vmem_limit_bytes=60 * 2**20),

time: 243 us -> 243 us (level)
  no operation moved by 1% of the time
where the time goes in v6:
time: 243 us; the launch traced here: 240 us
  Pallas kernels  240 us (99%)
    pallas_call x1, Pallas kernels, exchange(): pl.pallas_call(kernel, out_shape=(jax.ShapeDtypeStruct((NE, CAP, D), bf),...  233 us
    pallas_call x1, Pallas kernels, finish(): pl.pallas_call(finish_kernel, out_shape=(jax.ShapeDtypeStruct((TOK, D), b...  6.82 us

profile of v6, /device:TPU:67, one launch (start us, length us, event | category | flops | bytes accessed | tf_op | source)
XLA Modules:
  0.0 240.4 jit_solution(16355755960907734100)
XLA Ops:
  0.6 232.8 %shard_map.110 = (bf16[32,24,4096]{2,1,0:T(8,128)(2,1)}, bf16[32,24,4096]{2,1,0:T(8,128)(2,1)}, bf16[32,24,4096]{2,1,0:T(8,128)(2,1)}, bf16[256,4096]{1,0:T(8,12...) custom-call(s32[2,256]{1,0:T(2,128)} %bitcast.12, ...), custom_call_target="tpu_custom_call" | custom-call | tf_op jit(solution)/shard_map/pallas_call | solution.py:400
  233.4 6.8 %shard_map.111 = (bf16[256,4096]{1,0:T(8,128)(2,1)}, bf16[2,256]{1,0:T(2,128)(2,1)}, bf16[1024,512]{1,0:T(8,128)(2,1)}, bf16[1024,512]{1,0:T(8,128)(2,1)}, bf16[512,1024]{1,0:T(8,128)(2,1)}) custom-call(bf16[192,256]{1,0:T(8,128)(2,1)} %get-tuple-element.16.put_last, f32[2,256]{1,0:T(2,128)} %get-tuple-element.17.sums, ...), custom_call_target="tpu_custom_call" | custom-call | tf_op jit(solution)/shard_map/pallas_call | solution.py:491
